TPU v7x, 128 devices: a whole 4x4x4 slice. The times are simulated.
128 devices in a mesh: cell: 16 (over y, x), sub: 8 (over z, core).
Axes of the slice: x: 4, y: 4, z: 4, core: 2. Of those that a mesh axis runs over, the one named last changes fastest.
Arguments:
- source: float32 [512, 384, 256], P('cell', 'sub'), may hold values from -60 to 60
- permeability: float32 [512, 384, 256], P('cell', 'sub'), may hold values from 0.2 to 5
- storage: float32 [512, 384, 256], P('cell', 'sub'), may hold values from 1 to 10
- face_cell: int32 [262144], P(('cell', 'sub')), may hold values from 0 to 393215
- face_dest: int32 [262144, 1], P(('cell', 'sub')), may hold values from 0 to 127; in each aligned block of 2048 rows (0 to 2047, 2048 to 4095, ...) at most 32 rows name the same one
- face_dof: int32 [262144], P(('cell', 'sub')), may hold values from 0 to 3071
- face_weight: float32 [262144], P(('cell', 'sub')), may hold values from -6 to 6
- tectonic_load: float32 [512, 768], P(('cell', 'sub')), may hold values from -6 to 6
- patch_matrix: float32 [512, 768, 768], P(('cell', 'sub')), as said below
- yield_limit: float32 [512, 768], P(('cell', 'sub')), may hold values from 0.2 to 2
- free_mask: int32 [4, 512, 768], P(None, ('cell', 'sub')), may hold values 0 or 1
- step_kind: int32 [4, 512], P(None, ('cell', 'sub')), may hold values from 0 to 2
Outputs:
- pressure_change: float32 [512, 384, 256], P('cell', 'sub')
- slip: float32 [512, 768], P(('cell', 'sub'))
Inputs may be any that keep to these rules, and one draw needn't show every extreme that they name: `face_dest`: within the faces of one block (aligned blocks of 2048 rows) no owner is named more than 32 times, and in every draw some block names some owner exactly 32 times. `face_cell`: flattened index of the cell inside the block that holds the face. `face_dof`: index patch-major over the owner's 4 patches. `free_mask`: 1 marks a free unknown. `step_kind`: 0: conjugate step on the free unknowns, 1: proportioning step along the chopped gradient, 2: expansion step along the full gradient. `patch_matrix`: each patch's matrix is symmetric positive definite.
All inputs are finite; a program needn't handle non-finite values. No bound on the sum of `free_mask` on one device may be relied on, other than what follows from the above.
Results may differ from a plain program's by a relative error of at most 0.00011.
Values sent between devices are 32-bit elements; how exact they have to be, the bound alone decides.
No kernel may reach another device: no remote copies, remote signals or barrier semaphores. Data moves between devices by JAX's collectives and lax.ppermute only.
A program may use at most 128 MiB of HBM per device.

v0:
```python
import jax
import jax.numpy as jnp
from jax import lax
from jax.sharding import PartitionSpec as P

PRES_ITERS = 2
FRIC_ITERS = 4


HIGHEST = lax.Precision.HIGHEST


def with_halo(cells, sides, width):
    for axis, dim in sides:
        count = lax.axis_size(axis)
        ends = count - 1
        head = lax.slice_in_dim(cells, 0, width, axis=dim)
        tail = lax.slice_in_dim(cells, cells.shape[dim] - width, cells.shape[dim], axis=dim)
        cells = jnp.concatenate(
            [
                lax.ppermute(tail, axis, [(i, (i + 1) % count) for i in range(ends)]),
                cells,
                lax.ppermute(head, axis, [((i + 1) % count, i) for i in range(ends)]),
            ],
            axis=dim,
        )
    return cells


def harmonic(here_perm, there_perm):
    return 2.0 * here_perm * there_perm / (here_perm + there_perm)


def neighbours(padded):
    return (
        padded[2:, 1:-1, 1:-1],
        padded[:-2, 1:-1, 1:-1],
        padded[1:-1, 2:, 1:-1],
        padded[1:-1, :-2, 1:-1],
        padded[1:-1, 1:-1, 2:],
        padded[1:-1, 1:-1, :-2],
    )


def widen_depth(padded):
    return jnp.pad(padded, ((0, 0), (0, 0), (1, 1)))


def patch_solve(patch_matrix, fault_load, yield_limit, free_mask, step_kind):
    slip_now = jnp.zeros_like(fault_load)
    previous = jnp.zeros_like(fault_load)
    previous_image = jnp.zeros_like(fault_load)
    for iteration in range(FRIC_ITERS):
        gradient = jnp.einsum("pij,pj->pi", patch_matrix, slip_now, precision=HIGHEST) - fault_load
        free_now = free_mask[iteration].astype(jnp.float32)
        kind_now = step_kind[iteration][:, None]
        free_part = free_now * gradient
        chopped = (1.0 - free_now) * gradient
        conjugacy = jnp.mean(free_part * previous_image, axis=1, keepdims=True) / (
            jnp.mean(previous * previous_image, axis=1, keepdims=True) + 1e-06
        )
        direction = jnp.where(
            kind_now == 0,
            free_part - conjugacy * previous,
            jnp.where(kind_now == 1, chopped, gradient),
        )
        image_vec = jnp.einsum("pij,pj->pi", patch_matrix, direction, precision=HIGHEST)
        step_length = jnp.mean(gradient * direction, axis=1, keepdims=True) / (
            jnp.mean(direction * image_vec, axis=1, keepdims=True) + 1e-06
        )
        slip_now = jnp.clip(slip_now - step_length * direction, -yield_limit, yield_limit)
        previous = direction
        previous_image = image_vec
    return slip_now


def on_device(
    source,
    permeability,
    storage,
    face_cell,
    face_dest,
    face_dof,
    face_weight,
    tectonic_load,
    patch_matrix,
    yield_limit,
    free_mask,
    step_kind,
):
    perm_padded = widen_depth(with_halo(permeability, (("cell", 0), ("sub", 1)), 1))
    conductances = [harmonic(permeability, perm_side) for perm_side in neighbours(perm_padded)]

    def residual_norm(residual):
        return lax.psum(jnp.sum(residual * residual), ("cell", "sub"))

    pressure_change = jnp.zeros_like(source)
    residual = source
    direction = source
    norm_now = residual_norm(residual)
    for iteration in range(PRES_ITERS):
        padded = widen_depth(with_halo(direction, (("cell", 0), ("sub", 1)), 1))
        summed = storage * direction
        for conduct, near_value in zip(conductances, neighbours(padded)):
            summed = summed + conduct * (direction - near_value)
        step_length = norm_now / lax.psum(jnp.sum(direction * summed), ("cell", "sub"))
        pressure_change = pressure_change + step_length * direction
        if iteration + 1 < PRES_ITERS:
            residual = residual - step_length * summed
            norm_next = residual_norm(residual)
            direction = residual + norm_next / norm_now * direction
            norm_now = norm_next
    flattened = pressure_change.reshape(-1)
    face_values = face_weight * flattened[face_cell]
    owner_ids = face_dest[:, 0]
    patch_width = tectonic_load.shape[0] * tectonic_load.shape[1]
    devices = lax.axis_size(("cell", "sub"))
    load_terms = jax.ops.segment_sum(
        face_values, owner_ids * patch_width + face_dof, num_segments=devices * patch_width
    )
    fault_load = tectonic_load.reshape(-1) + lax.psum_scatter(
        load_terms, ("cell", "sub"), scatter_dimension=0, tiled=True
    )
    fault_load = fault_load.reshape(tectonic_load.shape)
    slip = patch_solve(patch_matrix, fault_load, yield_limit, free_mask, step_kind)
    return (pressure_change, slip)


def solution(mesh):
    return jax.shard_map(
        on_device,
        mesh=mesh,
        in_specs=(
            P("cell", "sub", None),
            P("cell", "sub", None),
            P("cell", "sub", None),
            P(("cell", "sub")),
            P(("cell", "sub"), None),
            P(("cell", "sub")),
            P(("cell", "sub")),
            P(("cell", "sub"), None),
            P(("cell", "sub"), None, None),
            P(("cell", "sub"), None),
            P(None, ("cell", "sub"), None),
            P(None, ("cell", "sub")),
        ),
        out_specs=(P("cell", "sub", None), P(("cell", "sub"), None)),
        check_vma=False,
    )
```

profile of v0, /device:TPU:1, one launch (start us, length us, event | category | flops | bytes accessed | tf_op | source)
XLA Modules:
  0.0 515.1 jit_solution(13430764606695750348)
XLA Ops:
  8.0 3.9 collective-permute-start.2
  14.1 4.0 collective-permute-start.3
  21.2 3.4 collective-permute-start.4
  24.6 3.4 collective-permute-start.6
  30.2 3.6 collective-permute-start.7
  38.0 6.4 %multiply_reduce_fusion.1 = (f32[]{:T(128)}, f32[]{:T(128)}, f32[32,48,256]{2,1,0:T(8,128)S(1)}) fusion(f32[32,48,256]{2,1,0:T(8,128)S(1)} %copy-done, f32[34,50,258]{2,1,0:T(8,128)S(1)} %select_maximum_fusion.4, f32[32,48,256]{2,1,0:T(8,128)S(1)} %copy-done.5, f32[34,50,258]{2,1,0:T(8,128)S(1)} %select_maximum_fusion.6, ...), kind=kLoop, calls=%fused_computation.77 | loop fusion | flops 19660800 | bytes 16261128 | tf_op jit(solution)/shard_map/reduce_sum | solution.py:106
  44.5 70.6 %all-reduce.4 = (f32[]{:T(128)}, f32[]{:T(128)}) all-reduce(f32[]{:T(128)} %get-tuple-element.3, f32[]{:T(128)} %get-tuple-element.2), channel_id=1, replica_groups=mesh['cell'=16,'sub'=8] {'cell','sub'}, use_global_device_ids=true, to_apply=%region_1.2 | all-reduce | flops 2 | bytes 16 | tf_op jit(solution)/shard_map/psum | solution.py:95
  117.5 62.9 %psum.30 = f32[]{:T(128)} all-reduce(f32[]{:T(128)} %multiply_reduce_fusion), channel_id=1, replica_groups=mesh['cell'=16,'sub'=8] {'cell','sub'}, use_global_device_ids=true, to_apply=%region_5.6 | all-reduce | flops 1 | bytes 8 | tf_op jit(solution)/shard_map/psum | solution.py:95
  183.5 4.0 collective-permute-start.9
  188.7 3.8 collective-permute-start.10
  192.5 2.9 collective-permute-start.11
  197.8 6.8 %fusion.4 = f32[]{:T(128)} fusion(f32[32,48,256]{2,1,0:T(8,128)S(1)} %multiply_add_fusion.1, f32[34,50,258]{2,1,0:T(8,128)S(1)} %select_maximum_fusion, f32[34,1,256]{2,1,0:T(1,128)S(1)} %collective-permute-done.11, f32[1,48,256]{2,1,0:T(8,128)S(1)} %collective-permute-done.8, f32[1,48,256]{2,1,0:T(8,128)S(1)} %collective-permute-done.9, ...), kind=kLoop, calls=%fused_computation.17 | loop fusion | flops 20447232 | bytes 13017092 | tf_op jit(solution)/shard_map/reduce_sum | solution.py:106
  204.7 67.1 %psum.31 = f32[]{:T(128)} all-reduce(f32[]{:T(128)} %fusion.4), channel_id=1, replica_groups=mesh['cell'=16,'sub'=8] {'cell','sub'}, use_global_device_ids=true, to_apply=%region_7.8 | all-reduce | flops 1 | bytes 8 | tf_op jit(solution)/shard_map/psum | solution.py:106
  274.6 11.8 %gather_fusion = f32[2048]{0:T(1024)S(1)} fusion(f32[393216]{0:T(1024)S(1)} %bitcast.131, s32[2048]{0:T(1024)S(1)} %fusion.68), kind=kCustom, calls=%fused_computation | custom fusion | bytes 24576 | tf_op jit(solution)/shard_map/gather | solution.py:114
  286.4 12.4 %scatter_custom_fusion = f32[393216]{0:T(1024)} fusion(s32[2048]{0:T(1024)S(1)} %add.159, f32[2048]{0:T(1024)S(1)} %mul.279, f32[]{:T(128)} %constant.34.clone.1), kind=kCustom, calls=%fused_computation.83 | custom fusion | flops 2048 | bytes 1572868 | tf_op jit(solution)/shard_map/scatter-add | solution.py:118
  299.0 9.8 %fusion.69 = f32[4,1,768]{2,1,0:T(1,128)S(1)} fusion(f32[4,768,768]{2,1,0:T(8,128)} %param.20), kind=kOutput, calls=%fused_computation.154 | convolution fusion | flops 28311552 | bytes 9449472 | tf_op jit(solution)/shard_map/pij,pj->pi/dot_general | solution.py:54
  308.8 136.0 %all-reduce.7.cloned.1.call-done = f32[393216]{0:T(1024)} async-done(((f32[393216]{0:T(1024)}), f32[393216]{0:T(1024)}) %all-reduce.7.cloned.1.call-update) | async-done | bytes 1572880
  445.8 10.0 %fusion.66 = f32[4,1,768]{2,1,0:T(1,128)S(1)} fusion(f32[4,768,768]{2,1,0:T(8,128)} %param.20, f32[4,768,1]{1,0,2:T(4,128)S(1)} %bitcast.133), kind=kOutput, calls=%fused_computation.142 | convolution fusion | flops 28311552 | bytes 9461760 | tf_op jit(solution)/shard_map/pij,pj->pi/dot_general | solution.py:67
  456.0 10.2 %fusion.64 = f32[4,1,768]{2,1,0:T(1,128)S(1)} fusion(f32[4,768,768]{2,1,0:T(8,128)} %param.20, f32[4,768,1]{1,0,2:T(4,128)S(1)} %fusion.72), kind=kOutput, calls=%fused_computation.140 | convolution fusion | flops 28311552 | bytes 9461760 | tf_op jit(solution)/shard_map/pij,pj->pi/dot_general | solution.py:54
  466.5 7.8 %fusion.62 = f32[4,1,768]{2,1,0:T(1,128)S(1)} fusion(f32[4,768,768]{2,1,0:T(8,128)S(1)} %bitcast.130, f32[4,768,1]{1,0,2:T(4,128)S(1)} %bitcast.135), kind=kOutput, calls=%fused_computation.138 | convolution fusion | flops 28311552 | bytes 9461760 | tf_op jit(solution)/shard_map/pij,pj->pi/dot_general | solution.py:67
  474.6 8.2 %fusion.60 = f32[4,1,768]{2,1,0:T(1,128)S(1)} fusion(f32[4,768,768]{2,1,0:T(8,128)S(1)} %bitcast.130, f32[4,768,1]{1,0,2:T(4,128)S(1)} %bitcast.136), kind=kOutput, calls=%fused_computation.136 | convolution fusion | flops 28311552 | bytes 9461760 | tf_op jit(solution)/shard_map/pij,pj->pi/dot_general | solution.py:54
  483.0 7.9 %fusion.58 = f32[4,1,768]{2,1,0:T(1,128)S(1)} fusion(f32[4,768,768]{2,1,0:T(8,128)S(1)} %bitcast.130, f32[4,768,1]{1,0,2:T(4,128)S(1)} %bitcast.134), kind=kOutput, calls=%fused_computation.134 | convolution fusion | flops 28311552 | bytes 9461760 | tf_op jit(solution)/shard_map/pij,pj->pi/dot_general | solution.py:67
  491.1 8.0 %fusion.56 = f32[4,1,768]{2,1,0:T(1,128)S(1)} fusion(f32[4,768,768]{2,1,0:T(8,128)S(1)} %bitcast.130, f32[4,768,1]{1,0,2:T(4,128)S(1)} %fusion.73), kind=kOutput, calls=%fused_computation.132 | convolution fusion | flops 28311552 | bytes 9461760 | tf_op jit(solution)/shard_map/pij,pj->pi/dot_general | solution.py:54
  499.4 7.9 %fusion.54 = f32[4,1,768]{2,1,0:T(1,128)S(1)} fusion(f32[4,768,768]{2,1,0:T(8,128)S(1)} %bitcast.130, f32[4,768,1]{1,0,2:T(4,128)S(1)} %bitcast.137), kind=kOutput, calls=%fused_computation.130 | convolution fusion | flops 28311552 | bytes 9461760 | tf_op jit(solution)/shard_map/pij,pj->pi/dot_general | solution.py:67
  (112 shorter events, 23.2 us)
Async XLA Ops:
  7.2 437.6 %all-reduce.7.cloned.1.call-start = ((), (), s32[]{:S(2)}) async-start(), calls=%async_computation | async-start | bytes 3145728
  8.0 11.4 %collective-permute-start.2 = (f32[1,48,256]{2,1,0:T(8,128)S(1)}, f32[1,48,256]{2,1,0:T(8,128)S(1)}, u32[]{:S(2)}, u32[]{:S(2)}) collective-permute-start(f32[1,48,256]{2,1,0:T(8,128)S(1)} %get-tuple-element.24), channel_id=1, source_target_pairs={{0,8},{8,16},{16,24},{24,32},{32,40},{40,48},{48,56},{56,64},{64,7... | collective-permute-start | bytes 147464 | tf_op jit(solution)/shard_map/ppermute | solution.py:21
  12.0 9.1 %collective-permute-start = (f32[1,48,256]{2,1,0:T(8,128)S(1)}, f32[1,48,256]{2,1,0:T(8,128)S(1)}, u32[]{:S(2)}, u32[]{:S(2)}) collective-permute-start(f32[1,48,256]{2,1,0:T(8,128)S(1)} %get-tuple-element.23), channel_id=1, source_target_pairs={{8,0},{16,8},{24,16},{32,24},{40,32},{48,40},{56,48},{64,56},{72,6... | collective-permute-start | bytes 147464 | tf_op jit(solution)/shard_map/ppermute | solution.py:23
  14.1 13.9 %collective-permute-start.3 = (f32[1,48,256]{2,1,0:T(8,128)S(1)}, f32[1,48,256]{2,1,0:T(8,128)S(1)}, u32[]{:S(2)}, u32[]{:S(2)}) collective-permute-start(f32[1,48,256]{2,1,0:T(8,128)S(1)} %get-tuple-element.26), channel_id=1, source_target_pairs={{0,8},{8,16},{16,24},{24,32},{32,40},{40,48},{48,56},{56,64},{64,7... | collective-permute-start | bytes 147464 | tf_op jit(solution)/shard_map/ppermute | solution.py:21
  18.1 10.1 %collective-permute-start.1 = (f32[1,48,256]{2,1,0:T(8,128)S(1)}, f32[1,48,256]{2,1,0:T(8,128)S(1)}, u32[]{:S(2)}, u32[]{:S(2)}) collective-permute-start(f32[1,48,256]{2,1,0:T(8,128)S(1)} %get-tuple-element.25), channel_id=1, source_target_pairs={{8,0},{16,8},{24,16},{32,24},{40,32},{48,40},{56,48},{64,56},{72,6... | collective-permute-start | bytes 147464 | tf_op jit(solution)/shard_map/ppermute | solution.py:23
  21.1 15.2 %copy-start.3 = (f32[34,48,256]{2,1,0:T(8,128)}, f32[34,48,256]{2,1,0:T(8,128)S(1)}, u32[]{:S(2)}) copy-start(f32[34,48,256]{2,1,0:T(8,128)S(1)} %constant_dynamic-update-slice_fusion) | copy-start | bytes 5013508
  21.2 12.7 %collective-permute-start.4 = (f32[34,1,256]{2,1,0:T(1,128)S(1)}, f32[34,1,256]{2,1,0:T(1,128)S(1)}, u32[]{:S(2)}, u32[]{:S(2)}) collective-permute-start(f32[34,1,256]{2,1,0:T(1,128)S(1)} %get-tuple-element.18), channel_id=1, source_target_pairs={{1,0},{2,1},{3,2},{4,3},{5,4},{6,5},{7,6},{9,8},{10,9},{11,10},{12... | collective-permute-start | bytes 104456 | tf_op jit(solution)/shard_map/ppermute | solution.py:23
  24.6 9.3 %collective-permute-start.6 = (f32[34,1,256]{2,1,0:T(1,128)S(1)}, f32[34,1,256]{2,1,0:T(1,128)S(1)}, u32[]{:S(2)}, u32[]{:S(2)}) collective-permute-start(f32[34,1,256]{2,1,0:T(1,128)S(1)} %get-tuple-element.17), channel_id=1, source_target_pairs={{0,1},{1,2},{2,3},{3,4},{4,5},{5,6},{6,7},{8,9},{9,10},{10,11},{11... | collective-permute-start | bytes 104456 | tf_op jit(solution)/shard_map/ppermute | solution.py:21
  28.3 6.8 %collective-permute-start.5 = (f32[34,1,256]{2,1,0:T(1,128)S(1)}, f32[34,1,256]{2,1,0:T(1,128)S(1)}, u32[]{:S(2)}, u32[]{:S(2)}) collective-permute-start(f32[34,1,256]{2,1,0:T(1,128)S(1)} %get-tuple-element.20), channel_id=1, source_target_pairs={{1,0},{2,1},{3,2},{4,3},{5,4},{6,5},{7,6},{9,8},{10,9},{11,10},{12... | collective-permute-start | bytes 104456 | tf_op jit(solution)/shard_map/ppermute | solution.py:23
  30.2 4.9 collective-permute-start.7
  181.7 16.0 %copy-start.9 = (f32[32,48,256]{2,1,0:T(8,128)S(1)}, f32[32,48,256]{2,1,0:T(8,128)}, u32[]{:S(2)}) copy-start(f32[32,48,256]{2,1,0:T(8,128)} %param.14) | copy-start | bytes 4718596
  182.0 13.4 %copy-start.16 = (s32[2048]{0:T(1024)S(1)}, s32[2048]{0:T(1024)}, u32[]{:S(2)}) copy-start(s32[2048]{0:T(1024)} %param.15) | copy-start | bytes 24580
  182.1 5.5 %collective-permute-start.8 = (f32[1,48,256]{2,1,0:T(8,128)S(1)}, f32[1,48,256]{2,1,0:T(8,128)S(1)}, u32[]{:S(2)}, u32[]{:S(2)}) collective-permute-start(f32[1,48,256]{2,1,0:T(8,128)S(1)} %get-tuple-element.22), channel_id=1, source_target_pairs={{8,0},{16,8},{24,16},{32,24},{40,32},{48,40},{56,48},{64,56},{72,6... | collective-permute-start | bytes 147464 | tf_op jit(solution)/shard_map/ppermute | solution.py:23
  183.5 5.2 %collective-permute-start.9 = (f32[1,48,256]{2,1,0:T(8,128)S(1)}, f32[1,48,256]{2,1,0:T(8,128)S(1)}, u32[]{:S(2)}, u32[]{:S(2)}) collective-permute-start(f32[1,48,256]{2,1,0:T(8,128)S(1)} %get-tuple-element.21), channel_id=1, source_target_pairs={{0,8},{8,16},{16,24},{24,32},{32,40},{40,48},{48,56},{56,64},{64,7... | collective-permute-start | bytes 147464 | tf_op jit(solution)/shard_map/ppermute | solution.py:21
  188.7 6.8 %collective-permute-start.10 = (f32[34,1,256]{2,1,0:T(1,128)S(1)}, f32[34,1,256]{2,1,0:T(1,128)S(1)}, u32[]{:S(2)}, u32[]{:S(2)}) collective-permute-start(f32[34,1,256]{2,1,0:T(1,128)S(1)} %get-tuple-element.16), channel_id=1, source_target_pairs={{1,0},{2,1},{3,2},{4,3},{5,4},{6,5},{7,6},{9,8},{10,9},{11,10},{12... | collective-permute-start | bytes 104456 | tf_op jit(solution)/shard_map/ppermute | solution.py:23
  192.5 3.9 collective-permute-start.11
  274.6 11.8 %copy-start.14 = (f32[2048]{0:T(1024)S(1)}, f32[2048]{0:T(1024)}, u32[]{:S(2)}) copy-start(f32[2048]{0:T(1024)} %param.18) | copy-start | bytes 24580
  286.4 12.5 %copy-start.12 = (f32[4,768]{1,0:T(4,128)S(1)}, f32[4,768]{1,0:T(4,128)}, u32[]{:S(2)}) copy-start(f32[4,768]{1,0:T(4,128)} %param.19) | copy-start | bytes 36868
  286.4 12.5 %copy-start.17 = (s32[4,4]{1,0:T(4,128)S(1)}, s32[4,4]{1,0:T(4,128)}, u32[]{:S(2)}) copy-start(s32[4,4]{1,0:T(4,128)} %param.23) | copy-start | bytes 196
  298.9 146.6 %copy-start.11 = (s32[4,4,768]{2,1,0:T(4,128)S(1)}, s32[4,4,768]{2,1,0:T(4,128)}, u32[]{:S(2)}) copy-start(s32[4,4,768]{2,1,0:T(4,128)} %param.22) | copy-start | bytes 147460
  445.7 10.2 %copy-start.10 = (f32[4,768]{1,0:T(4,128)S(1)}, f32[4,768]{1,0:T(4,128)}, u32[]{:S(2)}) copy-start(f32[4,768]{1,0:T(4,128)} %param.21) | copy-start | bytes 36868
  445.7 20.7 %slice-start = ((s8[9437184]{0:T(1024)(128)(4,1)}), s8[4194304]{0:T(1024)(128)(4,1)S(1)}, s32[]{:S(2)}) async-start(s8[9437184]{0:T(1024)(128)(4,1)} %bitcast.129), calls=%async_computation.1 | async-start | bytes 8388608
  445.7 20.7 %slice-start.1 = ((s8[9437184]{0:T(1024)(128)(4,1)}), s8[4194304]{0:T(1024)(128)(4,1)S(1)}, s32[]{:S(2)}) async-start(s8[9437184]{0:T(1024)(128)(4,1)} %bitcast.129), calls=%async_computation.2 | async-start | bytes 8388608
  456.0 10.4 %slice-start.2 = ((s8[9437184]{0:T(1024)(128)(4,1)}), s8[1048576]{0:T(1024)(128)(4,1)S(1)}, s32[]{:S(2)}) async-start(s8[9437184]{0:T(1024)(128)(4,1)} %bitcast.129), calls=%async_computation.3 | async-start | bytes 2097152
  (10 other events, 43.0 us)
Sparse Core Ops, SparseCore 0:
  299.0 145.7 all-reduce.6
where the time goes:
time: 524 us; the launch traced here: 515 us
  blocking collectives  201 us (38%)
  waiting for transfers between devices  138 us (26%)
  matrix products  69.8 us (13%)
  starting transfers between devices  35.1 us (7%)
  other arithmetic  34.3 us (7%)
  between operations  18.9 us (4%)
  local copies, waits for them, and re-layouts  18.3 us (3%)
    unnamed x2, waiting for transfers between devices  136 us
    psum x2, blocking collectives, residual_norm(): return lax.psum(jnp.sum(residual * residual), ('cell', 'sub'))  134 us
    psum x1, blocking collectives, on_device(): lax.psum(jnp.sum(direction * summed), ('cell', 'sub'))  67.1 us
    dot_general x4, matrix products, patch_solve(): jnp.einsum('pij,pj->pi', patch_matrix, slip_now, precision=HIGHEST)  36.3 us
    dot_general x4, matrix products, patch_solve(): jnp.einsum('pij,pj->pi', patch_matrix, direction, precision=HIGHEST)  33.6 us
    ppermute x6, starting transfers between devices, with_halo(): lax.ppermute(tail, axis, [(i, (i + 1) % count) for i in range(ends)])  21.9 us
    reduce_sum x2, other arithmetic, on_device(): jnp.sum(direction * summed)  13.3 us
    ppermute x6, starting transfers between devices, with_halo(): lax.ppermute(head, axis, [((i + 1) % count, i) for i in range(ends)])  13.2 us
  transfers between devices with their start and end apart: 13, of which 3 were waited for; matrix products, arithmetic and copies ran while one was open for 3% of the time, Pallas kernels for 0%

commit v1 on v0

v1 whole, which is shorter than its diff:
```python
import functools

import jax
import jax.numpy as jnp
from jax import lax
from jax.experimental import pallas as pl
from jax.experimental.pallas import tpu as pltpu
from jax.sharding import PartitionSpec as P

SLOTS = 32
AXES = ("cell", "sub")
LANES = 128


def split3(values):
    first = values.astype(jnp.bfloat16).astype(jnp.float32)
    left = values - first
    second = left.astype(jnp.bfloat16).astype(jnp.float32)
    return first, second, left - second


def to_columns(block):
    return block.T


def onehot(values):
    return values.astype(jnp.float32).astype(jnp.bfloat16)


def pick_lane(gathered, lane_column):
    lane = lax.broadcasted_iota(jnp.int32, gathered.shape, 1).astype(jnp.float32)
    return jnp.sum(jnp.where(lane == lane_column, gathered, 0.0), axis=1, keepdims=True)


def grouped_pieces(value, rank):
    lane = lax.broadcasted_iota(jnp.int32, (value.shape[0], LANES), 1)
    first, second, third = split3(value)
    piece = jnp.where(lane < SLOTS, first, jnp.where(lane < 2 * SLOTS, second, third))
    here = ((lane & (SLOTS - 1)).astype(jnp.float32) == rank) & (lane < 3 * SLOTS)
    return jnp.where(here, piece, 0.0).astype(jnp.bfloat16)


def join_groups(summed, group):
    lane = lax.broadcasted_iota(jnp.int32, summed.shape, 1)
    joined = summed + pltpu.roll(summed, LANES - SLOTS, 1) + pltpu.roll(summed, LANES - 2 * SLOTS, 1)
    if group:
        joined = pltpu.roll(joined, group * SLOTS, 1)
    return jnp.where((lane >= group * SLOTS) & (lane < (group + 1) * SLOTS), joined, 0.0)


def copy_rows(table, picks, where_ref, first, count):
    for j in range(count):
        picks[pl.ds(first + j, 1), :] = table[pl.ds(where_ref[first + j], 1), :]


def faces_kernel(
    where_ref,
    dest_ref,
    code_ref,
    weight_ref,
    lane_ref,
    source_ref,
    sent_ref,
    columns_ref,
    table,
    picks,
    owners,
    spread,
    sems,
):
    chunks = dest_ref.shape[0]
    rows = source_ref.shape[0]
    halves = [
        pltpu.make_async_copy(
            source_ref.at[:, pl.ds(t * LANES, LANES)], table.at[pl.ds(t * rows, rows), :], sems.at[t]
        )
        for t in range(2)
    ]
    for half in halves:
        half.start()
    dest = dest_ref[...].astype(jnp.float32)
    dest_columns = to_columns(dest)
    code_columns = to_columns(code_ref[...])
    weight_columns = to_columns(weight_ref[...])
    lane_columns = to_columns(lane_ref[...].astype(jnp.float32))
    lane = lax.broadcasted_iota(jnp.int32, (LANES, LANES), 1)
    row = lax.broadcasted_iota(jnp.int32, (LANES, LANES), 0)
    lower = onehot(lane < row)
    lane_number = lane.astype(jnp.float32)
    start = jnp.zeros((1, LANES), jnp.float32)
    ranks = []
    for c in range(chunks):
        named = (lane_number == dest_columns[:, c : c + 1]).astype(jnp.float32)
        ahead = jnp.dot(lower, named.astype(jnp.bfloat16), preferred_element_type=jnp.float32)
        ranks.append(jnp.sum(named * (ahead + start), axis=1, keepdims=True))
        start = start + jnp.sum(named, axis=0, keepdims=True)
    columns_ref[...] = jnp.zeros_like(columns_ref)
    for c in range(chunks):
        columns_ref[:, c : c + 1] = ranks[c]
    columns_ref[:, chunks : 2 * chunks] = weight_columns
    columns_ref[:, 2 * chunks : 3 * chunks] = lane_columns
    for half in halves:
        half.wait()

    def gather(i, carry):
        copy_rows(table, picks, where_ref, i * 64, 64)
        return carry

    lax.fori_loop(0, chunks * LANES // 64, gather, 0)
    row_number = row.astype(jnp.float32)
    for c in range(chunks):
        span = pl.ds(c * LANES, LANES)
        owners[:, span] = onehot(row_number == dest[c : c + 1, :])
        value = weight_columns[:, c : c + 1] * pick_lane(picks[span, :], lane_columns[:, c : c + 1])
        spread[span, :LANES] = grouped_pieces(code_columns[:, c : c + 1], ranks[c])
        spread[span, LANES:] = grouped_pieces(value, ranks[c])
    summed = jnp.dot(owners[...], spread[...], preferred_element_type=jnp.float32)
    sent_ref[...] = join_groups(summed[:, :LANES], 0) + join_groups(summed[:, LANES:], 1)


def faces(source, where, lane, dest, code, weight):
    count = where.shape[0]
    chunks = count // LANES
    rows = source.shape[0] * source.shape[1]
    vmem = pl.BlockSpec(memory_space=pltpu.VMEM)
    cut = lambda values: values.reshape(chunks, LANES)
    return pl.pallas_call(
        faces_kernel,
        out_shape=(
            jax.ShapeDtypeStruct((LANES, LANES), jnp.float32),
            jax.ShapeDtypeStruct((LANES, LANES), jnp.float32),
        ),
        in_specs=[pl.BlockSpec(memory_space=pltpu.SMEM)] + [vmem] * 4 + [pl.BlockSpec(memory_space=pl.ANY)],
        out_specs=(vmem, vmem),
        scratch_shapes=[
            pltpu.VMEM((2 * rows, LANES), jnp.float32),
            pltpu.VMEM((count, LANES), jnp.float32),
            pltpu.VMEM((LANES, count), jnp.bfloat16),
            pltpu.VMEM((count, 2 * LANES), jnp.bfloat16),
            pltpu.SemaphoreType.DMA((2,)),
        ],
        compiler_params=pltpu.CompilerParams(vmem_limit_bytes=12 * 2**20),
        name="faces",
    )(where, cut(dest), cut(code), cut(weight), cut(lane), source.reshape(rows, source.shape[2]))


def image_kernel(
    where_ref,
    even_ref,
    dest_ref,
    columns_ref,
    sent_in_ref,
    cell_first_ref,
    cell_second_ref,
    sub_first_ref,
    sub_second_ref,
    source_ref,
    perm_ref,
    storage_ref,
    image_ref,
    sent_ref,
    field,
    half,
    store,
    image,
    flow_x,
    flow_y,
    flow_z,
    con_x,
    con_y,
    con_z,
    carry_x,
    table,
    picks,
    owners,
    spread,
    sems,
):
    planes, height, depth = source_ref.shape
    strips = height // 8
    group = 8
    copies = []
    for g in range(planes // group):
        for n, (array, held, shift) in enumerate(
            ((source_ref, field, 1), (perm_ref, half, 1), (storage_ref, store, 0))
        ):
            copies.append(
                pltpu.make_async_copy(
                    array.at[pl.ds(g * group, group)],
                    held.at[pl.ds(shift + g * group, group), pl.ds(8, height), :],
                    sems.at[3 * g + n],
                )
            )
    for copy in copies:
        copy.start()

    even_cell = even_ref[0] == 1
    even_sub = even_ref[1] == 1
    own = pl.ds(8, height)

    def cell_side(n):
        one, two = cell_first_ref[n], cell_second_ref[n]
        return jnp.where(even_cell, two, one), jnp.where(even_cell, one, two)

    lo, hi = cell_side(0)
    field[0, own, :] = lo
    field[planes + 1, own, :] = hi
    field[planes + 2, own, :] = cell_side(1)[1]
    lo, hi = cell_side(2)
    half[0, own, :] = lo
    half[planes + 1, own, :] = hi
    half[planes + 2, own, :] = cell_side(3)[1]
    store[planes, own, :] = cell_side(4)[1]

    def sub_side(n):
        one, two = sub_first_ref[n], sub_second_ref[n]
        return jnp.where(even_sub, two, one), jnp.where(even_sub, one, two)

    edge = 8 + height
    b_lo, b_hi = sub_side(0)
    b_far = sub_side(1)[1]
    k_lo, k_hi = sub_side(2)
    k_far = sub_side(3)[1]
    s_hi = sub_side(4)[1]
    for x in range(planes + 2):
        field[x, 7:8, :] = b_lo[x : x + 1]
        field[x, edge : edge + 1, :] = b_hi[x : x + 1]
        field[x, edge + 1 : edge + 2, :] = b_far[x : x + 1]
        half[x, 7:8, :] = k_lo[x : x + 1]
        half[x, edge : edge + 1, :] = k_hi[x : x + 1]
        half[x, edge + 1 : edge + 2, :] = k_far[x : x + 1]
        if x >= 1:
            store[x - 1, edge : edge + 1, :] = s_hi[x : x + 1]

    lane = lax.broadcasted_iota(jnp.int32, (8, depth), 1)
    row = lax.broadcasted_iota(jnp.int32, (8, depth), 0)

    def halve(x):
        half[x] = 0.5 / jnp.maximum(half[x], 1e-30)

    def first_x():
        for i in range(strips + 1):
            rows = pl.ds(8 + 8 * i, 8)
            conduct = 1.0 / (half[0, rows, :] + half[1, rows, :])
            carry_x[rows, :] = conduct * (field[0, rows, :] - field[1, rows, :])

    def plane(x, sums, inside):
        halve(x + 2)
        sums = list(sums)
        here_b, here_h = field[x + 1, 0:8, :], half[x + 1, 0:8, :]
        last_y = (here_b - field[x + 1, 1:9, :]) / (here_h + half[x + 1, 1:9, :])
        for i in range(strips + 1):
            at = 8 + 8 * i
            rows = pl.ds(at, 8)
            b, h, s = field[x + 1, rows, :], half[x + 1, rows, :], store[x, rows, :]
            if i < strips:
                b_y, h_y = field[x + 1, pl.ds(at + 1, 8), :], half[x + 1, pl.ds(at + 1, 8), :]
            else:
                b_y, h_y = pltpu.roll(b, 7, 0), pltpu.roll(h, 7, 0)
            b_x, h_x = field[x + 2, rows, :], half[x + 2, rows, :]
            c_x = 1.0 / (h + h_x)
            c_y = 1.0 / (h + h_y)
            c_z = jnp.where(lane == depth - 1, 0.0, 1.0 / (h + pltpu.roll(h, depth - 1, 1)))
            d_x, d_y, d_z = b - b_x, b - b_y, b - pltpu.roll(b, depth - 1, 1)
            f_x, f_y, f_z = c_x * d_x, c_y * d_y, c_z * d_z
            came_y = pltpu.roll(jnp.where(row == 7, last_y, f_y), 1, 0)
            sb = s * b
            w = sb + (f_x - carry_x[rows, :]) + (f_y - came_y) + (f_z - pltpu.roll(f_z, 1, 1))
            carry_x[rows, :] = f_x
            last_y = f_y
            image[x, rows, :] = w
            if inside and i < strips:
                out = pl.ds(8 * i, 8)
                image_ref[x, out, :] = w
                for t in range(2):
                    table[pl.ds(pl.multiple_of((t * planes + x) * height, 8) + 8 * i, 8), :] = w[
                        :, t * LANES : (t + 1) * LANES
                    ]
                con_x[x, out, :] = c_x
                con_y[x, out, :] = c_y
                con_z[x, out, :] = c_z
                flow_x[x, out, :] = f_x
                flow_y[x, out, :] = f_y
                flow_z[x, out, :] = f_z
                sums[0] = sums[0] + b * b
                sums[1] = sums[1] + b * w
                sums[2] = sums[2] + (sb * b + f_x * d_x) + (f_y * d_y + f_z * d_z)
        return tuple(sums)

    zero = jnp.zeros((8, depth), jnp.float32)
    sums = (zero, zero, zero)
    for g in range(planes // group):
        for copy in copies[3 * g : 3 * g + 3]:
            copy.wait()
        if g == 0:
            halve(0)
            halve(1)
            first_x()
        begin = 0 if g == 0 else g * group - 1
        end = planes - 1 if g == planes // group - 1 else (g + 1) * group - 1
        sums = lax.fori_loop(begin, end, lambda x, s: plane(x, s, True), sums)
    sums = plane(planes - 1, sums, True)
    plane(planes, sums, False)

    def total(values):
        return jnp.sum(jnp.sum(values, axis=1, keepdims=True), axis=0, keepdims=True)

    square, product, bb = [total(values) for values in sums]
    some = square > 0.0
    mu = jnp.where(some, product / jnp.where(some, square, 1.0), 0.0)

    def take_off(x, carry):
        for i in range(strips + 1):
            rows = pl.ds(8 + 8 * i, 8)
            image[x, rows, :] = image[x, rows, :] - mu * field[x + 1, rows, :]
        return carry

    lax.fori_loop(0, planes + 1, take_off, 0)
    each = where_ref.shape[0] // planes

    def rest(x, sums):
        vv, bv, vav = sums
        copy_rows(table, picks, where_ref, x * each, each)
        for i in range(strips):
            at = 8 + 8 * i
            rows, out = pl.ds(at, 8), pl.ds(8 * i, 8)
            v = image[x, rows, :]
            d_x = v - image[x + 1, rows, :]
            d_y = v - image[x, pl.ds(at + 1, 8), :]
            d_z = v - pltpu.roll(v, depth - 1, 1)
            sv = store[x, rows, :] * v
            vv = vv + v * v
            bv = bv + (sv * field[x + 1, rows, :] + flow_x[x, out, :] * d_x) + (
                flow_y[x, out, :] * d_y + flow_z[x, out, :] * d_z
            )
            vav = vav + (sv * v + con_x[x, out, :] * (d_x * d_x)) + (
                con_y[x, out, :] * (d_y * d_y) + con_z[x, out, :] * (d_z * d_z)
            )
        return vv, bv, vav

    vv, bv, vav = [total(values) for values in lax.fori_loop(0, planes, rest, (zero, zero, zero))]

    chunks = dest_ref.shape[0]
    dest = dest_ref[...]
    columns = columns_ref[...]
    owner = lax.broadcasted_iota(jnp.int32, (LANES, LANES), 0)
    for c in range(chunks):
        span = pl.ds(c * LANES, LANES)
        owners[:, span] = onehot(owner == dest[c : c + 1, :])
        value = columns[:, chunks + c : chunks + c + 1] * pick_lane(
            picks[span, :], columns[:, 2 * chunks + c : 2 * chunks + c + 1]
        )
        spread[span, :] = grouped_pieces(value, columns[:, c : c + 1])
    summed = jnp.dot(owners[...], spread[...], preferred_element_type=jnp.float32)
    sent = sent_in_ref[...] + join_groups(summed, 2)
    place = lax.broadcasted_iota(jnp.int32, sent.shape, 1)
    for n, scalar in enumerate((square, mu, vv, bb, bv, vav)):
        sent = jnp.where(place == 3 * SLOTS + n, scalar, sent)
    sent_ref[...] = sent


def apply_flow(where, even, dest, columns, sent, cells, subs, source, permeability, storage):
    planes, height, depth = source.shape
    count = where.shape[0]
    chunks = count // LANES
    vmem = pl.BlockSpec(memory_space=pltpu.VMEM)
    smem = pl.BlockSpec(memory_space=pltpu.SMEM)
    hbm = pl.BlockSpec(memory_space=pl.ANY)
    wide = lambda n: pltpu.VMEM((n, height + 16, depth), jnp.float32)
    block = pltpu.VMEM((planes, height, depth), jnp.float32)
    return pl.pallas_call(
        image_kernel,
        out_shape=(
            jax.ShapeDtypeStruct(source.shape, jnp.float32),
            jax.ShapeDtypeStruct((LANES, LANES), jnp.float32),
        ),
        in_specs=[smem, smem] + [vmem] * 7 + [hbm] * 3,
        out_specs=(vmem, vmem),
        scratch_shapes=[
            wide(planes + 3),
            wide(planes + 3),
            wide(planes + 1),
            wide(planes + 1),
        ]
        + [block] * 6
        + [
            pltpu.VMEM((height + 16, depth), jnp.float32),
            pltpu.VMEM((2 * planes * height, LANES), jnp.float32),
            pltpu.VMEM((count, LANES), jnp.float32),
            pltpu.VMEM((LANES, count), jnp.bfloat16),
            pltpu.VMEM((count, LANES), jnp.bfloat16),
            pltpu.SemaphoreType.DMA((3 * planes // 8,)),
        ],
        compiler_params=pltpu.CompilerParams(vmem_limit_bytes=36 * 2**20),
        name="image",
    )(where, even, dest.reshape(chunks, LANES), columns, sent, *cells, *subs, source, permeability, storage)


def final_kernel(
    steps,
    kind_ref,
    got_ref,
    tectonic_ref,
    yield_ref,
    free_ref,
    matrix_ref,
    source_ref,
    image_ref,
    pressure_ref,
    slip_ref,
    wide,
    tall,
    turned,
    rows,
):
    patches, unknowns = tectonic_ref.shape
    tiles = unknowns // LANES
    got = got_ref[...]
    across = got.T
    scal = [across[3 * SLOTS + i : 3 * SLOTS + i + 1, :] for i in range(6)]
    square, mu, rest_sq, bb, bv, vv = scal

    def total(row):
        return jnp.sum(row, axis=1, keepdims=True)

    norm = total(square)
    alpha = norm / total(bb)
    part = 1.0 - alpha * mu
    edge = part * jnp.sqrt(square)
    norm_next = total(edge * edge + alpha * alpha * rest_sq)
    beta = norm_next / norm
    part = part + beta
    curve = total(part * part * bb - 2.0 * part * alpha * bv + alpha * alpha * vv)
    alpha_next = norm_next / curve
    on_source = alpha + alpha_next * (1.0 + beta)
    on_image = -alpha_next * alpha

    count = got.shape[0]
    code = got[:, :SLOTS].astype(jnp.int32)
    code_across = across[:SLOTS].astype(jnp.int32)
    terms = on_source * across[SLOTS : 2 * SLOTS] + on_image * across[2 * SLOTS : 3 * SLOTS]
    pieces = split3(terms)
    lane = lax.broadcasted_iota(jnp.int32, (count, LANES), 1)
    high = lax.broadcasted_iota(jnp.int32, (8 * tiles, count), 0)
    low_code = code & (LANES - 1)
    high_code = code_across >> 7
    for slot in range(SLOTS):
        span = pl.ds(slot * count, count)
        wide[span, :] = (lane == low_code[:, slot : slot + 1]).astype(jnp.float32).astype(jnp.bfloat16)
        here = high == high_code[slot : slot + 1, :]
        for index, piece in enumerate(pieces):
            tall[pl.ds(index * 8 * tiles, 8 * tiles), span] = jnp.where(
                here, piece[slot : slot + 1, :], 0.0
            ).astype(jnp.bfloat16)
    summed = jnp.dot(tall[...], wide[...], preferred_element_type=jnp.float32)
    summed = summed[: 8 * tiles] + summed[8 * tiles : 16 * tiles] + summed[16 * tiles :]
    loads = jnp.concatenate([summed[8 * t : 8 * t + 8] for t in range(tiles)], axis=1)
    fault_load = tectonic_ref[...] + loads[:patches]

    for x in range(0, source_ref.shape[0], 4):
        pressure_ref[x : x + 4] = on_source[None] * source_ref[x : x + 4] + on_image[None] * image_ref[x : x + 4]

    piece_row = lax.broadcasted_iota(jnp.int32, (16, patches * LANES), 0)
    piece_lane = lax.broadcasted_iota(jnp.int32, (16, patches * LANES), 1)
    choose = onehot((piece_row & 3) == (piece_lane >> 7))

    def times_matrix(vector):
        pieces = jnp.concatenate([*split3(vector), jnp.zeros_like(vector)], axis=0)
        turned[...] = jnp.dot(
            pieces.T.astype(jnp.bfloat16), choose, preferred_element_type=jnp.float32
        )
        group = 8

        def body(i, sums):
            sums = list(sums)
            for g in range(group):
                start = pl.multiple_of(i * (8 * group), 8 * group) + 8 * g
                for p in range(patches):
                    spread = turned[pl.ds(start, 8), p * LANES : (p + 1) * LANES]
                    sums[p] = sums[p] + matrix_ref[p, pl.ds(start, 8), :] * jnp.concatenate(
                        [spread] * tiles, axis=1
                    )
            return tuple(sums)

        zero = jnp.zeros((8, unknowns), jnp.float32)
        sums = lax.fori_loop(0, unknowns // (8 * group), body, (zero,) * patches)
        for p in range(patches):
            rows[p : p + 1, :] = jnp.sum(sums[p], axis=0, keepdims=True)
        return rows[:patches, :]

    def mean(values):
        return jnp.sum(values, axis=1, keepdims=True) * (1.0 / unknowns)

    limit = yield_ref[...]
    row = lax.broadcasted_iota(jnp.int32, (patches, unknowns), 0)
    slip_now = None
    previous = None
    previous_image = None
    for iteration in range(steps):
        if iteration == 0:
            gradient = -fault_load
        else:
            gradient = times_matrix(slip_now) - fault_load
        free_part = jnp.where(free_ref[iteration] == 1, gradient, 0.0)
        kind = jnp.zeros((patches, unknowns), jnp.int32)
        for p in range(patches):
            kind = jnp.where(row == p, kind_ref[iteration, p], kind)
        conjugate = free_part
        if iteration > 0:
            conjugacy = mean(free_part * previous_image) / (mean(previous * previous_image) + 1e-06)
            conjugate = free_part - conjugacy * previous
        direction = jnp.where(
            kind == 0, conjugate, jnp.where(kind == 1, gradient - free_part, gradient)
        )
        image_vec = times_matrix(direction)
        step_length = mean(gradient * direction) / (mean(direction * image_vec) + 1e-06)
        moved = -step_length * direction if iteration == 0 else slip_now - step_length * direction
        slip_now = jnp.clip(moved, -limit, limit)
        previous = direction
        previous_image = image_vec
    slip_ref[...] = slip_now


def finish(got, tectonic_load, yield_limit, free_mask, step_kind, patch_matrix, source, image):
    patches, unknowns = tectonic_load.shape
    tiles = unknowns // LANES
    count = got.shape[0]
    vmem = pl.BlockSpec(memory_space=pltpu.VMEM)
    return pl.pallas_call(
        functools.partial(final_kernel, step_kind.shape[0]),
        out_shape=(
            jax.ShapeDtypeStruct(source.shape, jnp.float32),
            jax.ShapeDtypeStruct(tectonic_load.shape, jnp.float32),
        ),
        in_specs=[pl.BlockSpec(memory_space=pltpu.SMEM)] + [vmem] * 7,
        out_specs=(vmem, vmem),
        scratch_shapes=[
            pltpu.VMEM((SLOTS * count, LANES), jnp.bfloat16),
            pltpu.VMEM((24 * tiles, SLOTS * count), jnp.bfloat16),
            pltpu.VMEM((unknowns, patches * LANES), jnp.float32),
            pltpu.VMEM((8, unknowns), jnp.float32),
        ],
        compiler_params=pltpu.CompilerParams(vmem_limit_bytes=20 * 2**20),
        name="finish",
    )(step_kind, got, tectonic_load, yield_limit, free_mask, patch_matrix, source, image)


def swap_pairs(head, tail, axis):
    count = lax.axis_size(axis)
    even = lax.axis_index(axis) % 2 == 0
    first = [(i, i ^ 1) for i in range(count)]
    second = [(i, i + 1) for i in range(1, count - 1, 2)]
    second = second + [(j, i) for i, j in second]
    return (
        lax.ppermute(jnp.where(even, tail, head), axis, first),
        lax.ppermute(jnp.where(even, head, tail), axis, second),
    )


def load_code(face_dof, unknowns):
    patch, unknown = face_dof // unknowns, face_dof % unknowns
    return ((unknown // LANES * 8 + patch) * LANES + unknown % LANES).astype(jnp.float32)


def on_device(
    source,
    permeability,
    storage,
    face_cell,
    face_dest,
    face_dof,
    face_weight,
    tectonic_load,
    patch_matrix,
    yield_limit,
    free_mask,
    step_kind,
):
    planes, height, depth = source.shape
    even_cell = lax.axis_index("cell") % 2 == 0
    even_sub = lax.axis_index("sub") % 2 == 0
    head = jnp.stack([source[0], source[1], permeability[0], permeability[1], storage[0]])
    tail = jnp.stack([source[-1], source[-2], permeability[-1], permeability[-2], storage[-1]])
    cells = swap_pairs(head, tail, "cell")
    before = jnp.where(even_cell, cells[1], cells[0])
    after = jnp.where(even_cell, cells[0], cells[1])

    def rows(near, far):
        def column(array, plane, y):
            return jnp.concatenate([before[plane, y][None], array[:, y], after[plane, y][None]])

        return jnp.stack(
            [
                column(source, 0, near),
                column(source, 0, far),
                column(permeability, 2, near),
                column(permeability, 2, far),
                column(storage, 4, near),
            ]
        )

    subs = swap_pairs(rows(0, 1), rows(height - 1, height - 2), "sub")

    where = (face_cell >> 7) % 2 * (planes * height) + (face_cell >> 8)
    dest = face_dest[:, 0]
    sent, columns = faces(
        source, where, face_cell & (LANES - 1), dest, load_code(face_dof, tectonic_load.shape[1]), face_weight
    )
    even = jnp.stack([even_cell, even_sub]).astype(jnp.int32)
    image, sent = apply_flow(where, even, dest, columns, sent, cells, subs, source, permeability, storage)
    got = lax.all_to_all(sent, AXES, 0, 0, tiled=True)
    pressure_change, slip = finish(
        got, tectonic_load, yield_limit, free_mask, step_kind, patch_matrix, source, image
    )
    return (pressure_change, slip)


def solution(mesh):
    return jax.shard_map(
        on_device,
        mesh=mesh,
        in_specs=(
            P("cell", "sub", None),
            P("cell", "sub", None),
            P("cell", "sub", None),
            P(("cell", "sub")),
            P(("cell", "sub"), None),
            P(("cell", "sub")),
            P(("cell", "sub")),
            P(("cell", "sub"), None),
            P(("cell", "sub"), None, None),
            P(("cell", "sub"), None),
            P(None, ("cell", "sub"), None),
            P(None, ("cell", "sub")),
        ),
        out_specs=(P("cell", "sub", None), P(("cell", "sub"), None)),
        check_vma=False,
    )
```

time: 524 us -> 86.2 us (0.16); the launches traced: 515 us -> 85.5 us
  blocking collectives: 201 us -> 19.7 us
  waiting for transfers between devices: 138 us -> 0.01 us
  matrix products: 69.8 us -> 0 us
  Pallas kernels: 0 us -> 37.1 us
  other arithmetic: 34.3 us -> 4.3 us
  starting transfers between devices: 35.1 us -> 9.98 us
  between operations: 18.9 us -> 0.92 us
    psum x3 -> x0, blocking collectives: 201 us -> none  [the longest x2 134 us: residual_norm(): return lax.psum(jnp.sum(residual * residual), ('cell', 'sub'))]
    unnamed x2 -> x0, waiting for transfers between devices: 136 us -> none
    dot_general x8 -> x0, matrix products: 69.8 us -> none  [the longest x4 36.3 us: patch_solve(): jnp.einsum('pij,pj->pi', patch_matrix, slip_now, precision=HIGHEST)]
    pallas_call x0 -> x3, Pallas kernels: none -> 37.1 us  [the longest x1 14.7 us: apply_flow(): pl.pallas_call(image_kernel, out_shape=(jax.ShapeDtypeStruct(source.shape...]
    ppermute x12 -> x4, starting transfers between devices: 35.1 us -> 9.98 us  [the longest x2 5.33 us: swap_pairs(): lax.ppermute(jnp.where(even, head, tail), axis, second)]
    all_to_all x0 -> x1, blocking collectives: none -> 19.7 us  [on_device(): got = lax.all_to_all(sent, AXES, 0, 0, tiled=True)]
    reduce_sum x11 -> x0, other arithmetic: 15.5 us -> none  [the longest x2 13.3 us: on_device(): jnp.sum(direction * summed)]
    scatter-add x1 -> x0, other arithmetic: 12.4 us -> none  [on_device(): jax.ops.segment_sum(face_values, owner_ids * patch_width + face_dof, num_...]
  transfers between devices with their start and end apart: 13 -> 4, of which waited for: 3 -> 0; matrix products, arithmetic and copies ran while one was open for 3% -> 7% of each run, Pallas kernels for 0% -> 12%
where the time goes in v1:
time: 86.2 us; the launch traced here: 85.5 us
  Pallas kernels  37.1 us (43%)
  blocking collectives  19.7 us (23%)
  local copies, waits for them, and re-layouts  13.5 us (16%)
  starting transfers between devices  9.98 us (12%)
  other arithmetic  4.3 us (5%)
  between operations  0.92 us (1%)
    all_to_all x1, blocking collectives, on_device(): got = lax.all_to_all(sent, AXES, 0, 0, tiled=True)  19.7 us
    pallas_call x1, Pallas kernels, apply_flow(): pl.pallas_call(image_kernel, out_shape=(jax.ShapeDtypeStruct(source.shape...  14.7 us
    pallas_call x1, Pallas kernels, finish(): pl.pallas_call(functools.partial(final_kernel, step_kind.shape[0]), out_s...  12.2 us
    pallas_call x1, Pallas kernels, faces(): pl.pallas_call(faces_kernel, out_shape=(jax.ShapeDtypeStruct((LANES, LANE...  10.2 us
    unnamed x30, local copies, waits for them, and re-layouts  6.19 us
    ppermute x2, starting transfers between devices, swap_pairs(): lax.ppermute(jnp.where(even, head, tail), axis, second)  5.33 us
    ppermute x2, starting transfers between devices, swap_pairs(): lax.ppermute(jnp.where(even, tail, head), axis, first)  4.65 us
    slice x3, local copies, waits for them, and re-layouts, column(): array[:, y]  3.13 us
  transfers between devices with their start and end apart: 4, of which 0 were waited for; matrix products, arithmetic and copies ran while one was open for 7% of the time, Pallas kernels for 12%

profile of v1, /device:TPU:1, one launch (start us, length us, event | category | flops | bytes accessed | tf_op | source)
XLA Modules:
  0.0 85.5 jit_solution(11266779808007070577)
XLA Ops:
  0.6 1.0 %slice.123 = f32[2,48,256]{2,1,0:T(8,128)S(1)} slice(f32[32,48,256]{2,1,0:T(8,128)} %source_ref.3), slice={[0:2], [0:48], [0:256]} | slice | bytes 196608 | tf_op jit(solution)/shard_map/slice | solution.py:582
  1.7 0.8 slice_dynamic-update-slice_fusion.4
  2.5 0.9 %slice.124 = f32[2,48,256]{2,1,0:T(8,128)S(1)} slice(f32[32,48,256]{2,1,0:T(8,128)} %perm_ref.1), slice={[0:2], [0:48], [0:256]} | slice | bytes 196608 | tf_op jit(solution)/shard_map/slice | solution.py:582
  3.4 0.8 slice_dynamic-update-slice_fusion.3
  4.2 0.8 slice_dynamic-update-slice_fusion.2
  5.0 0.8 slice_dynamic-update-slice_fusion.1
  5.8 0.8 fusion.30
  6.6 0.8 fusion
  8.1 4.6 %collective-permute-start = (f32[5,48,256]{2,1,0:T(8,128)}, f32[5,48,256]{2,1,0:T(8,128)}, u32[]{:S(2)}, u32[]{:S(2)}) collective-permute-start(f32[5,48,256]{2,1,0:T(8,128)} %get-tuple-element.25), channel_id=1, source_target_pairs={{0,8},{8,0},{16,24},{24,16},{32,40},{40,32},{48,56},{56,48},{64,72... | collective-permute-start | bytes 737288 | tf_op jit(solution)/shard_map/ppermute | solution.py:555
  12.7 1.1 %fusion.27 = (f32[32,1,256]{2,1,0:T(1,128)S(1)}, f32[32,1,256]{2,1,0:T(1,128)S(1)}) fusion(f32[32,48,256]{2,1,0:T(8,128)} %storage_ref.1), kind=kLoop, calls=%fused_computation.92 | loop fusion | bytes 131072 | tf_op jit(solution)/shard_map/slice | solution.py:590
  13.8 1.3 %fusion.28 = (f32[32,1,256]{2,1,0:T(1,128)S(1)}, f32[32,1,256]{2,1,0:T(1,128)S(1)}, f32[32,1,256]{2,1,0:T(1,128)S(1)}, f32[32,1,256]{2,1,0:T(1,128)S(1)}) fusion(f32[32,48,256]{2,1,0:T(8,128)} %perm_ref.1), kind=kLoop, calls=%fused_computation.93 | loop fusion | bytes 262144 | tf_op jit(solution)/shard_map/slice | solution.py:590
  15.1 0.7 fusion.29
  16.6 0.8 copy.55
  17.3 0.8 copy.56
  18.1 0.8 copy_bitcast_fusion.3
  18.9 1.1 %broadcast_select_fusion.1 = (f32[5,48,256]{2,1,0:T(8,128)S(1)}, f32[5,48,256]{2,1,0:T(8,128)S(1)}) fusion(f32[5,48,256]{2,1,0:T(8,128)S(1)} %collective-permute-done.1.cell_second_ref, f32[5,48,256]{2,1,0:T(8,128)} %collective-permute-done.cell_first_ref, pred[]{:T(512)} %eq.17), kind=kLoop, calls=%fused_computation.4 | loop fusion | flops 122880 | bytes 983041 | tf_op jit(solution)/shard_map/jit(_where)/select_n | solution.py:585
  20.1 1.0 %fusion.4 = f32[5,34,256]{2,1,0:T(8,128)S(1)} fusion(f32[5,34,256]{2,1,0:T(8,128)S(1)} %fusion.3, f32[1,256]{1,0:T(1,128)S(1)} %get-tuple-element.45, f32[32,256]{1,0:T(8,128)} %get-tuple-element.57, f32[1,256]{1,0:T(1,128)S(1)} %get-tuple-element.35), kind=kLoop, calls=%fused_computation.17 | loop fusion | flops 17408 | bytes 75776
  21.1 1.1 %fusion.5 = f32[5,34,256]{2,1,0:T(8,128)S(1)} fusion(f32[5,34,256]{2,1,0:T(8,128)S(1)} %fusion.4, f32[1,256]{1,0:T(1,128)S(1)} %get-tuple-element.44, f32[32,256]{1,0:T(8,128)} %get-tuple-element.56, f32[1,256]{1,0:T(1,128)S(1)} %get-tuple-element.34), kind=kLoop, calls=%fused_computation.19 | loop fusion | flops 17408 | bytes 75776
  22.4 4.7 %collective-permute-start.3 = (f32[5,34,256]{2,1,0:T(8,128)S(1)}, f32[5,34,256]{2,1,0:T(8,128)S(1)}, u32[]{:S(2)}, u32[]{:S(2)}) collective-permute-start(f32[5,34,256]{2,1,0:T(8,128)S(1)} %get-tuple-element.26), channel_id=1, source_target_pairs={{1,2},{3,4},{5,6},{2,1},{4,3},{6,5},{9,10},{11,12},{13,14},{10,9},... | collective-permute-start | bytes 522248 | tf_op jit(solution)/shard_map/ppermute | solution.py:556
  27.2 10.2 %faces.1 = (f32[128,128]{1,0:T(8,128)S(1)}, f32[128,128]{1,0:T(8,128)S(1)}) custom-call(s32[2048]{0:T(1024)S(1)} %get-tuple-element.49.where_ref, s32[16,128]{1,0:T(8,128)S(1)} %bitcast.118, f32[16,128]{1,0:T(8,128)S(1)} %fusion.20.code_ref, f32[16,128]{1,0:T(8,128)S(1)} %bitcast.120, s32[16,128]{1,0:T(8,128)S(1)} %get-tuple-element.48.lane_ref, ...), custom_call_target="tpu_custom_call" | custom-call | tf_op jit(solution)/shard_map/faces/pallas_call | solution.py:127
  37.4 1.4 %copy-done.3 = f32[32,48,256]{2,1,0:T(8,128)S(1)} copy-done((f32[32,48,256]{2,1,0:T(8,128)S(1)}, f32[32,48,256]{2,1,0:T(8,128)}, u32[]{:S(2)}) %copy-start.3) | copy-done | bytes 1572888
  38.8 14.7 %image.1 = (f32[32,48,256]{2,1,0:T(8,128)S(1)}, f32[128,128]{1,0:T(8,128)S(1)}) custom-call(s32[2048]{0:T(1024)S(1)} %get-tuple-element.49.where_ref, s32[2]{0:T(128)S(1)} %add_convert_fusion.even_ref, s32[16,128]{1,0:T(8,128)S(1)} %bitcast.119, f32[128,128]{1,0:T(8,128)S(1)} %get-tuple-element.6.columns_ref, f32[128,128]{1,0:T(8,128)S(1)} %get-tuple-element.7.sent_in_ref, ...), custom_call_target="tpu_custom_call" | custom-call | tf_op jit(solution)/shard_map/image/pallas_call | solution.py:371
  53.6 19.7 %all_to_all.11 = f32[128,1,128]{2,1,0:T(1,128)S(1)} all-to-all(f32[128,1,128]{2,1,0:T(1,128)S(1)} %bitcast.117), channel_id=1, replica_groups=mesh['cell'=16,'sub'=8] {'cell','sub'}, dimensions={0} | all-to-all | bytes 131072 | tf_op jit(solution)/shard_map/all_to_all | solution.py:611
  73.3 12.2 %finish.1 = (f32[32,48,256]{2,1,0:T(8,128)}, f32[4,768]{1,0:T(4,128)}) custom-call(s32[4,4]{1,0:T(4,128)S(1)} %copy-done.9, f32[128,128]{1,0:T(8,128)S(1)} %bitcast.116, f32[4,768]{1,0:T(4,128)S(1)} %copy-done.6, f32[4,768]{1,0:T(4,128)S(1)} %copy-done.7, s32[4,4,768]{2,1,0:T(4,128)S(1)} %copy-done.4, f32[4,768,768]{2,1,0:T(8,128)S(1)} %copy-done.1, ...), custom_call_target="tpu_custom_call" | custom-call | tf_op jit(solution)/shard_map/finish/pallas_call | solution.py:529
  (45 shorter events, 1.7 us)
Async XLA Ops:
  0.6 14.5 %copy-start = (f32[32,48,256]{2,1,0:T(8,128)S(1)}, f32[32,48,256]{2,1,0:T(8,128)}, u32[]{:S(2)}) copy-start(f32[32,48,256]{2,1,0:T(8,128)} %source_ref.3) | copy-start | bytes 4718596
  2.5 14.1 %copy-start.11 = (s32[2048]{0:T(1024)S(1)}, s32[2048]{0:T(1024)}, u32[]{:S(2)}) copy-start(s32[2048]{0:T(1024)} %param.17) | copy-start | bytes 24580
  7.5 11.4 %collective-permute-start.1 = (f32[5,48,256]{2,1,0:T(8,128)}, f32[5,48,256]{2,1,0:T(8,128)S(1)}, u32[]{:S(2)}, u32[]{:S(2)}) collective-permute-start(f32[5,48,256]{2,1,0:T(8,128)} %get-tuple-element.24), channel_id=1, source_target_pairs={{8,16},{24,32},{40,48},{56,64},{72,80},{88,96},{104,112},{16,8},{3... | collective-permute-start | bytes 737288 | tf_op jit(solution)/shard_map/ppermute | solution.py:556
  8.1 10.8 %collective-permute-start = (f32[5,48,256]{2,1,0:T(8,128)}, f32[5,48,256]{2,1,0:T(8,128)}, u32[]{:S(2)}, u32[]{:S(2)}) collective-permute-start(f32[5,48,256]{2,1,0:T(8,128)} %get-tuple-element.25), channel_id=1, source_target_pairs={{0,8},{8,0},{16,24},{24,16},{32,40},{40,32},{48,56},{56,48},{64,72... | collective-permute-start | bytes 737288 | tf_op jit(solution)/shard_map/ppermute | solution.py:555
  13.8 13.3 %copy-start.10 = (s32[2048]{0:T(1024)S(1)}, s32[2048]{0:T(1024)}, u32[]{:S(2)}) copy-start(s32[2048]{0:T(1024)} %param.15) | copy-start | bytes 24580
  13.8 13.4 %copy-start.5 = (s32[2048,1]{0,1:T(1,128)S(1)}, s32[2048,1]{0,1:T(1,128)}, u32[]{:S(2)}) copy-start(s32[2048,1]{0,1:T(1,128)} %param.16) | copy-start | bytes 24580
  13.8 13.4 %copy-start.8 = (f32[2048]{0:T(1024)S(1)}, f32[2048]{0:T(1024)}, u32[]{:S(2)}) copy-start(f32[2048]{0:T(1024)} %param.18) | copy-start | bytes 24580
  15.1 22.3 %copy-start.2 = (f32[32,48,256]{2,1,0:T(8,128)S(1)}, f32[32,48,256]{2,1,0:T(8,128)}, u32[]{:S(2)}) copy-start(f32[32,48,256]{2,1,0:T(8,128)} %perm_ref.1) | copy-start | bytes 4718596
  18.9 54.4 %copy-start.1 = (f32[4,768,768]{2,1,0:T(8,128)S(1)}, f32[4,768,768]{2,1,0:T(8,128)}, u32[]{:S(2)}) copy-start(f32[4,768,768]{2,1,0:T(8,128)} %matrix_ref.1) | copy-start | bytes 28311556
  22.4 15.1 %collective-permute-start.3 = (f32[5,34,256]{2,1,0:T(8,128)S(1)}, f32[5,34,256]{2,1,0:T(8,128)S(1)}, u32[]{:S(2)}, u32[]{:S(2)}) collective-permute-start(f32[5,34,256]{2,1,0:T(8,128)S(1)} %get-tuple-element.26), channel_id=1, source_target_pairs={{1,2},{3,4},{5,6},{2,1},{4,3},{6,5},{9,10},{11,12},{13,14},{10,9},... | collective-permute-start | bytes 522248 | tf_op jit(solution)/shard_map/ppermute | solution.py:556
  27.0 10.4 %collective-permute-start.2 = (f32[5,34,256]{2,1,0:T(8,128)S(1)}, f32[5,34,256]{2,1,0:T(8,128)S(1)}, u32[]{:S(2)}, u32[]{:S(2)}) collective-permute-start(f32[5,34,256]{2,1,0:T(8,128)S(1)} %get-tuple-element.27), channel_id=1, source_target_pairs={{0,1},{1,0},{2,3},{3,2},{4,5},{5,4},{6,7},{7,6},{8,9},{9,8},{10,11... | collective-permute-start | bytes 522248 | tf_op jit(solution)/shard_map/ppermute | solution.py:555
  37.4 1.4 %copy-start.3 = (f32[32,48,256]{2,1,0:T(8,128)S(1)}, f32[32,48,256]{2,1,0:T(8,128)}, u32[]{:S(2)}) copy-start(f32[32,48,256]{2,1,0:T(8,128)} %storage_ref.1) | copy-start | bytes 4718596
  38.8 34.5 %copy-start.4 = (s32[4,4,768]{2,1,0:T(4,128)S(1)}, s32[4,4,768]{2,1,0:T(4,128)}, u32[]{:S(2)}) copy-start(s32[4,4,768]{2,1,0:T(4,128)} %free_ref.1) | copy-start | bytes 147460
  38.8 34.5 %copy-start.6 = (f32[4,768]{1,0:T(4,128)S(1)}, f32[4,768]{1,0:T(4,128)}, u32[]{:S(2)}) copy-start(f32[4,768]{1,0:T(4,128)} %tectonic_ref.1) | copy-start | bytes 36868
  38.8 34.5 %copy-start.7 = (f32[4,768]{1,0:T(4,128)S(1)}, f32[4,768]{1,0:T(4,128)}, u32[]{:S(2)}) copy-start(f32[4,768]{1,0:T(4,128)} %yield_ref.1) | copy-start | bytes 36868
  38.8 34.5 %copy-start.9 = (s32[4,4]{1,0:T(4,128)S(1)}, s32[4,4]{1,0:T(4,128)}, u32[]{:S(2)}) copy-start(s32[4,4]{1,0:T(4,128)} %kind_ref.1) | copy-start | bytes 196

commit v2 on v1

v2 whole, which is shorter than its diff:
```python
import functools

import jax
import jax.numpy as jnp
from jax import lax
from jax.experimental import pallas as pl
from jax.experimental.pallas import tpu as pltpu
from jax.sharding import PartitionSpec as P

SLOTS = 32
AXES = ("cell", "sub")
LANES = 128
EDGES = 61 * 2**20
INSIDE = 46 * 2**20
UNROLL = 2


def split3(values):
    first = values.astype(jnp.bfloat16).astype(jnp.float32)
    left = values - first
    second = left.astype(jnp.bfloat16).astype(jnp.float32)
    return first, second, left - second


def onehot(values):
    return values.astype(jnp.float32).astype(jnp.bfloat16)


def dot(left, right):
    return jnp.dot(left, right, preferred_element_type=jnp.float32)


def pieces_of(values):
    return jnp.concatenate([piece.astype(jnp.bfloat16) for piece in split3(values)], axis=1)


def spread_columns(columns, chunks):
    shape = (columns.shape[1], chunks * LANES)
    take = lax.broadcasted_iota(jnp.int32, shape, 0) % chunks == lax.broadcasted_iota(jnp.int32, shape, 1) // LANES
    return dot(columns, onehot(take))


def sum_lanes(values):
    return dot(pieces_of(values), jnp.ones((3 * LANES, LANES), jnp.bfloat16))


def grouped_pieces(value, slots):
    lane = lax.broadcasted_iota(jnp.int32, value.shape, 1)
    first, second, third = split3(value)
    piece = jnp.where(lane < SLOTS, first, jnp.where(lane < 2 * SLOTS, second, third))
    return jnp.where(slots > 0.0, piece, 0.0).astype(jnp.bfloat16)


def join_groups(summed, group):
    lane = lax.broadcasted_iota(jnp.int32, summed.shape, 1)
    joined = summed + pltpu.roll(summed, LANES - SLOTS, 1) + pltpu.roll(summed, LANES - 2 * SLOTS, 1)
    if group:
        joined = pltpu.roll(joined, group * SLOTS, 1)
    return jnp.where((lane >= group * SLOTS) & (lane < (group + 1) * SLOTS), joined, 0.0)


def copy_rows(table, picks, where_ref, first, count):
    for j in range(count):
        picks[pl.ds(first + j, 1), :] = table[pl.ds(where_ref[first + j], 1), :]


def faces_kernel(
    where_ref,
    dest_ref,
    code_ref,
    weight_ref,
    lane_ref,
    source_ref,
    sent_ref,
    slots_ref,
    picker_ref,
    table,
    picks,
    owners,
    spread,
    sems,
):
    chunks = dest_ref.shape[0]
    rows = source_ref.shape[0]
    halves = [
        pltpu.make_async_copy(
            source_ref.at[:, pl.ds(t * LANES, LANES)], table.at[pl.ds(t * rows, rows), :], sems.at[t]
        )
        for t in range(2)
    ]
    for half in halves:
        half.start()
    dest = dest_ref[...].astype(jnp.float32)
    lane = lax.broadcasted_iota(jnp.int32, (LANES, LANES), 1)
    row = lax.broadcasted_iota(jnp.int32, (LANES, LANES), 0)
    lower = onehot(lane < row)
    lane_number = lane.astype(jnp.float32)
    row_number = row.astype(jnp.float32)
    ones = jnp.ones((LANES, LANES), jnp.bfloat16)
    dest_spread = spread_columns(dest.T.astype(jnp.bfloat16), chunks)
    lane_spread = spread_columns(lane_ref[...].astype(jnp.float32).T.astype(jnp.bfloat16), chunks)
    weight_spread = spread_columns(pieces_of(weight_ref[...].T), chunks)
    code_spread = spread_columns(pieces_of(code_ref[...].T), chunks)
    start = jnp.zeros((1, LANES), jnp.float32)
    for c in range(chunks):
        span = pl.ds(c * LANES, LANES)
        cut = slice(c * LANES, (c + 1) * LANES)
        named = (lane_number == dest_spread[:, cut]).astype(jnp.float32)
        ahead = dot(lower, named.astype(jnp.bfloat16))
        rank = dot((named * (ahead + start)).astype(jnp.bfloat16), ones)
        start = start + jnp.sum(named, axis=0, keepdims=True)
        here = ((lane & (SLOTS - 1)).astype(jnp.float32) == rank) & (lane < 3 * SLOTS)
        slots = here.astype(jnp.float32)
        slots_ref[:, span] = slots.astype(jnp.bfloat16)
        picker_ref[:, span] = jnp.where(lane_number == lane_spread[:, cut], weight_spread[:, cut], 0.0)
        owners[:, span] = onehot(row_number == dest[c : c + 1, :])
        spread[span, :LANES] = grouped_pieces(code_spread[:, cut], slots)
    for half in halves:
        half.wait()

    def gather(i, carry):
        copy_rows(table, picks, where_ref, i * 64, 64)
        return carry

    lax.fori_loop(0, chunks * LANES // 64, gather, 0)
    for c in range(chunks):
        span = pl.ds(c * LANES, LANES)
        value = sum_lanes(picks[span, :] * picker_ref[:, span])
        spread[span, LANES:] = grouped_pieces(value, slots_ref[:, span].astype(jnp.float32))
    summed = dot(owners[...], spread[...])
    sent_ref[...] = join_groups(summed[:, :LANES], 0) + join_groups(summed[:, LANES:], 1)


def faces(source, where, lane, dest, code, weight):
    count = where.shape[0]
    chunks = count // LANES
    rows = source.shape[0] * source.shape[1]
    vmem = pl.BlockSpec(memory_space=pltpu.VMEM)
    cut = lambda values: values.reshape(chunks, LANES)
    return pl.pallas_call(
        faces_kernel,
        out_shape=(
            jax.ShapeDtypeStruct((LANES, LANES), jnp.float32),
            jax.ShapeDtypeStruct((LANES, count), jnp.bfloat16),
            jax.ShapeDtypeStruct((LANES, count), jnp.float32),
        ),
        in_specs=[pl.BlockSpec(memory_space=pltpu.SMEM)] + [vmem] * 4 + [pl.BlockSpec(memory_space=pltpu.HBM)],
        out_specs=(vmem, vmem, vmem),
        scratch_shapes=[
            pltpu.VMEM((2 * rows, LANES), jnp.float32),
            pltpu.VMEM((count, LANES), jnp.float32),
            pltpu.VMEM((LANES, count), jnp.bfloat16),
            pltpu.VMEM((count, 2 * LANES), jnp.bfloat16),
            pltpu.SemaphoreType.DMA((2,)),
        ],
        compiler_params=pltpu.CompilerParams(vmem_limit_bytes=12 * 2**20),
        name="faces",
    )(where, cut(dest), cut(code), cut(weight), cut(lane), source.reshape(rows, source.shape[2]))


def image_kernel(
    source_ref,
    perm_ref,
    storage_ref,
    image_ref,
    con_x_ref,
    con_y_ref,
    con_z_ref,
    sums_ref,
    first_ref,
    second_ref,
    field,
    half,
    store,
    carry_x,
    sems,
):
    planes, height, depth = source_ref.shape
    strips = height // 8
    group = 8
    copies = []
    for g in range(planes // group):
        span = pl.ds(g * group, group)
        for n, (array, held) in enumerate(((source_ref, field), (perm_ref, half), (storage_ref, store))):
            copies.append(pltpu.make_async_copy(array.at[span], held.at[span], sems.at[3 * g + n]))
    for copy in copies:
        copy.start()
    lane = lax.broadcasted_iota(jnp.int32, (8, depth), 1)
    row = lax.broadcasted_iota(jnp.int32, (8, depth), 0)
    zero = jnp.zeros((8, depth), jnp.float32)

    even = is_even("sub")
    for out in (first_ref, second_ref):
        for n in range(len(WANTED)):
            out[n, 0:8, :] = zero
            out[n, planes : planes + 8, :] = zero

    def send_rows(x):
        for k, out in enumerate((first_ref, second_ref)):
            at_end = even if k == 0 else 1 - even
            for n, (f, deep) in enumerate(WANTED):
                row = deep + at_end * (height - 1 - 2 * deep)
                out[n, pl.ds(x + 1, 1), :] = (field, half, store)[f][x, pl.ds(row, 1), :]

    def plane(x, sums, last):
        if not last:
            send_rows(x + 1)
            half[x + 1] = half_of(half[x + 1])
        square, product = sums
        last_y = zero
        for i in range(strips):
            at = 8 * i
            rows = pl.ds(at, 8)
            b, h = field[x, rows, :], half[x, rows, :]
            if i + 1 < strips:
                b_y, h_y = field[x, pl.ds(at + 1, 8), :], half[x, pl.ds(at + 1, 8), :]
                c_y = 1.0 / (h + h_y)
            else:
                b_y, h_y = pltpu.roll(b, 7, 0), pltpu.roll(h, 7, 0)
                c_y = jnp.where(row == 7, 0.0, 1.0 / (h + h_y))
            c_z = jnp.where(lane == depth - 1, 0.0, 1.0 / (h + pltpu.roll(h, depth - 1, 1)))
            f_y, f_z = c_y * (b - b_y), c_z * (b - pltpu.roll(b, depth - 1, 1))
            came_y = pltpu.roll(jnp.where(row == 7, last_y, f_y), 1, 0)
            last_y = f_y
            w = store[x, rows, :] * b + (f_y - came_y) + (f_z - pltpu.roll(f_z, 1, 1)) - carry_x[rows, :]
            if last:
                c_x = zero
            else:
                c_x = 1.0 / (h + half[x + 1, rows, :])
                f_x = c_x * (b - field[x + 1, rows, :])
                carry_x[rows, :] = f_x
                w = w + f_x
            image_ref[x, rows, :] = w
            con_x_ref[x, rows, :] = c_x
            con_y_ref[x, rows, :] = c_y
            con_z_ref[x, rows, :] = c_z
            square = square + b * b
            product = product + b * w
        return square, product

    sums = (zero, zero)
    chunks = planes // group
    for copy in copies[:3]:
        copy.wait()
    send_rows(0)
    half[0] = half_of(half[0])
    carry_x[...] = jnp.zeros_like(carry_x)
    for g in range(chunks):
        for copy in copies[3 * g + 3 : 3 * g + 6]:
            copy.wait()
        runs = group // UNROLL if g + 1 < chunks else group // UNROLL - 1

        def run(n, sums):
            for u in range(UNROLL):
                sums = plane(g * group + n * UNROLL + u, sums, False)
            return sums

        sums = lax.fori_loop(0, runs, run, sums)
    for x in range(planes - UNROLL, planes - 1):
        sums = plane(x, sums, False)
    square, product = plane(planes - 1, sums, True)
    sums_ref[0] = square
    sums_ref[1] = product


def half_of(perm):
    return 0.5 / jnp.maximum(perm, 1e-30)


def image_inside(source, permeability, storage):
    planes, height, depth = source.shape
    vmem = pl.BlockSpec(memory_space=pltpu.VMEM)
    block = jax.ShapeDtypeStruct(source.shape, jnp.float32)
    held = pltpu.VMEM(source.shape, jnp.float32)
    line = jax.ShapeDtypeStruct((5, planes + 8, depth), jnp.float32)
    return pl.pallas_call(
        image_kernel,
        out_shape=(block,) * 4 + (jax.ShapeDtypeStruct((2, 8, depth), jnp.float32), line, line),
        in_specs=[pl.BlockSpec(memory_space=pl.ANY)] * 3,
        out_specs=(vmem,) * 7,
        scratch_shapes=[
            held,
            held,
            held,
            pltpu.VMEM((height, depth), jnp.float32),
            pltpu.SemaphoreType.DMA((3 * planes // 8,)),
        ],
        compiler_params=pltpu.CompilerParams(vmem_limit_bytes=INSIDE),
        name="image",
    )(source, permeability, storage)


def norms_kernel(
    where_ref,
    dest_ref,
    slots_ref,
    picker_ref,
    sent_in_ref,
    side_first_ref,
    side_second_ref,
    cell_first_ref,
    cell_second_ref,
    line_first_ref,
    line_second_ref,
    sub_first_ref,
    sub_second_ref,
    part_ref,
    con_x_ref,
    con_y_ref,
    con_z_ref,
    sums_ref,
    source_ref,
    storage_ref,
    image_ref,
    sent_ref,
    rest,
    flows,
    lines,
    table,
    picks,
    owners,
    spread,
):
    planes, height, depth = source_ref.shape
    strips = height // 8
    even_cell = is_even("cell") == 1
    even_sub = is_even("sub") == 1

    def total(values):
        return jnp.sum(jnp.sum(values, axis=1, keepdims=True), axis=0, keepdims=True)

    def conduct(one, other):
        return 1.0 / (half_of(one) + half_of(other))

    def along_depth(b, k):
        lane = lax.broadcasted_iota(jnp.int32, b.shape, 1)
        flow = conduct(k, pltpu.roll(k, depth - 1, 1)) * (b - pltpu.roll(b, depth - 1, 1))
        flow = jnp.where(lane == depth - 1, 0.0, flow)
        return flow - pltpu.roll(flow, 1, 1)

    def cell_side(n):
        one, two = cell_first_ref[n], cell_second_ref[n]
        return jnp.where(even_cell, two, one), jnp.where(even_cell, one, two)

    def own_side(n):
        one, two = side_first_ref[n], side_second_ref[n]
        return jnp.where(even_cell, two, one), jnp.where(even_cell, one, two)

    b_lo, b_hi = cell_side(0)
    b_far = cell_side(1)[1]
    k_lo, k_hi = cell_side(2)
    k_far = cell_side(3)[1]
    s_hi = cell_side(4)[1]
    b_head, b_tail = own_side(0)
    k_head, k_tail = own_side(2)
    con_hi = conduct(k_tail, k_hi)
    flow_lo = conduct(k_lo, k_head) * (b_lo - b_head)
    flow_hi = con_hi * (b_tail - b_hi)

    def sub_side(n):
        one, two = sub_first_ref[n], sub_second_ref[n]
        return jnp.where(even_sub, two, one), jnp.where(even_sub, one, two)

    def own_line(n):
        one, two = line_first_ref[n], line_second_ref[n]
        return jnp.where(even_sub, two, one), jnp.where(even_sub, one, two)

    by_lo, by_hi = sub_side(0)
    by_far = sub_side(1)[1]
    ky_lo, ky_hi = sub_side(2)
    ky_far = sub_side(3)[1]
    sy_hi = sub_side(4)[1]
    by_head, by_tail = own_line(0)
    ky_head, ky_tail = own_line(2)
    cony_hi = conduct(ky_tail, ky_hi)
    flowy_lo = conduct(ky_lo, ky_head) * (by_lo - by_head)
    flowy_hi = cony_hi * (by_tail - by_hi)
    count = by_lo.shape[0]
    number = lax.broadcasted_iota(jnp.int32, by_lo.shape, 0)
    inside = (number >= 1) & (number <= planes)

    row = lax.broadcasted_iota(jnp.int32, b_hi.shape, 0)
    flow = conduct(k_hi, pltpu.roll(k_hi, height - 1, 0)) * (b_hi - pltpu.roll(b_hi, height - 1, 0))
    flow = jnp.where(row == height - 1, flowy_hi[planes + 1 : planes + 2], flow)
    came = jnp.where(row == 0, flowy_lo[planes + 1 : planes + 2], pltpu.roll(flow, 1, 0))
    w_hi = s_hi * b_hi + (conduct(k_hi, k_far) * (b_hi - b_far) - flow_hi) + (flow - came)
    w_hi = w_hi + along_depth(b_hi, k_hi)

    flow = conduct(ky_hi, pltpu.roll(ky_hi, count - 1, 0)) * (by_hi - pltpu.roll(by_hi, count - 1, 0))
    wy_hi = sy_hi * by_hi + (conduct(ky_hi, ky_far) * (by_hi - by_far) - flowy_hi)
    wy_hi = wy_hi + (flow - pltpu.roll(flow, 1, 0)) + along_depth(by_hi, ky_hi)

    def rows_total(values):
        return total(jnp.where(inside, values, 0.0))

    square = total(sums_ref[0])
    lower = total(flow_lo * b_head) + rows_total(flowy_lo * by_head)
    product = total(sums_ref[1]) - lower + total(flow_hi * b_tail) + rows_total(flowy_hi * by_tail)
    bb = product - total(flow_hi * b_hi) - rows_total(flowy_hi * by_hi) + lower
    some = square > 0.0
    mu = jnp.where(some, product / jnp.where(some, square, 1.0), 0.0)

    flows[0] = flowy_lo
    flows[1] = flowy_hi
    lines[...] = jnp.zeros_like(lines)
    strip_row = lax.broadcasted_iota(jnp.int32, (8, depth), 0)

    def complete(x, extra):
        for i in range(strips):
            rows = pl.ds(8 * i, 8)
            w = part_ref[x, rows, :]
            if extra is not None:
                w = w + extra[8 * i : 8 * i + 8]
            if i == 0:
                w = w - jnp.where(strip_row == 0, flows[0, pl.ds(x + 1, 1), :], 0.0)
            if i == strips - 1:
                w = w + jnp.where(strip_row == 7, flows[1, pl.ds(x + 1, 1), :], 0.0)
            image_ref[x, rows, :] = w
            for t in range(2):
                table[pl.ds(pl.multiple_of((t * planes + x) * height, 8) + 8 * i, 8), :] = w[
                    :, t * LANES : (t + 1) * LANES
                ]
            v = w - mu * source_ref[x, rows, :]
            rest[x, rows, :] = v
            if i == 0:
                lines[0, pl.ds(x + 1, 1), :] = v[0:1]
            if i == strips - 1:
                lines[1, pl.ds(x + 1, 1), :] = v[7:8]

    complete(0, -flow_lo)

    def middle(x, carry):
        complete(x, None)
        return carry

    lax.fori_loop(1, planes - 1, middle, 0)
    complete(planes - 1, flow_hi)
    v_hi = w_hi - mu * b_hi
    vy_hi = wy_hi - mu * by_hi
    rest[planes] = v_hi

    each = where_ref.shape[0] // planes

    def measure(x, sums):
        vv, vav = sums
        copy_rows(table, picks, where_ref, x * each, each)
        for i in range(strips):
            rows = pl.ds(8 * i, 8)
            v = rest[x, rows, :]
            d_x = v - rest[x + 1, rows, :]
            if i + 1 < strips:
                d_y = v - rest[x, pl.ds(8 * i + 1, 8), :]
            else:
                d_y = v - pltpu.roll(v, 7, 0)
            d_z = v - pltpu.roll(v, depth - 1, 1)
            squared = v * v
            vv = vv + squared
            vav = vav + (storage_ref[x, rows, :] * squared + con_x_ref[x, rows, :] * (d_x * d_x)) + (
                con_y_ref[x, rows, :] * (d_y * d_y) + con_z_ref[x, rows, :] * (d_z * d_z)
            )
        return vv, vav

    zero = jnp.zeros((8, depth), jnp.float32)
    vv, vav = [total(values) for values in lax.fori_loop(0, planes, measure, (zero, zero))]
    v_head, v_tail = rest[0], rest[planes - 1]
    vy_head, vy_tail = lines[0], lines[1]
    bv = vv - total(flow_hi * v_hi) - rows_total(flowy_hi * vy_hi)
    bv = bv + total(flow_lo * v_head) + rows_total(flowy_lo * vy_head)
    vav = vav + total(con_hi * ((v_tail - v_hi) * (v_tail - v_hi)))
    vav = vav + rows_total(cony_hi * ((vy_tail - vy_hi) * (vy_tail - vy_hi)))

    chunks = dest_ref.shape[0]
    dest = dest_ref[...]
    owner = lax.broadcasted_iota(jnp.int32, (LANES, LANES), 0)
    for c in range(chunks):
        span = pl.ds(c * LANES, LANES)
        owners[:, span] = onehot(owner == dest[c : c + 1, :])
        value = sum_lanes(picks[span, :] * picker_ref[:, span])
        spread[span, :] = grouped_pieces(value, slots_ref[:, span].astype(jnp.float32))
    summed = dot(owners[...], spread[...])
    sent = sent_in_ref[...] + join_groups(summed, 2)
    place = lax.broadcasted_iota(jnp.int32, sent.shape, 1)
    for n, scalar in enumerate((square, mu, vv, bb, bv, vav)):
        sent = jnp.where(place == 3 * SLOTS + n, scalar, sent)
    sent_ref[...] = sent


def norms(where, dest, marks, sides, cells, lines, subs, inner, source, storage):
    planes, height, depth = source.shape
    count = where.shape[0]
    chunks = count // LANES
    vmem = pl.BlockSpec(memory_space=pltpu.VMEM)
    smem = pl.BlockSpec(memory_space=pltpu.SMEM)
    line = pltpu.VMEM((2,) + lines[0].shape[1:], jnp.float32)
    operands = (dest.reshape(chunks, LANES), *marks, *sides, *cells, *lines, *subs, *inner, source, storage)
    return pl.pallas_call(
        norms_kernel,
        out_shape=(
            jax.ShapeDtypeStruct(source.shape, jnp.float32),
            jax.ShapeDtypeStruct((LANES, LANES), jnp.float32),
        ),
        in_specs=[smem] + [vmem] * len(operands),
        out_specs=(vmem, vmem),
        scratch_shapes=[
            pltpu.VMEM((planes + 1, height, depth), jnp.float32),
            line,
            line,
            pltpu.VMEM((2 * planes * height, LANES), jnp.float32),
            pltpu.VMEM((count, LANES), jnp.float32),
            pltpu.VMEM((LANES, count), jnp.bfloat16),
            pltpu.VMEM((count, LANES), jnp.bfloat16),
        ],
        compiler_params=pltpu.CompilerParams(vmem_limit_bytes=16 * 2**20),
        name="norms",
    )(where, *operands)


def final_kernel(
    steps,
    kind_ref,
    got_ref,
    tectonic_ref,
    yield_ref,
    free_ref,
    matrix_ref,
    source_ref,
    image_ref,
    pressure_ref,
    slip_ref,
    pressure,
    wide,
    tall,
    turned,
    rows,
    sem,
):
    patches, unknowns = tectonic_ref.shape
    tiles = unknowns // LANES
    got = got_ref[...]
    across = got.T
    scal = [across[3 * SLOTS + i : 3 * SLOTS + i + 1, :] for i in range(6)]
    square, mu, rest_sq, bb, bv, vv = scal

    def total(row):
        return jnp.sum(row, axis=1, keepdims=True)

    norm = total(square)
    alpha = norm / total(bb)
    part = 1.0 - alpha * mu
    edge = part * jnp.sqrt(square)
    norm_next = total(edge * edge + alpha * alpha * rest_sq)
    beta = norm_next / norm
    part = part + beta
    curve = total(part * part * bb - 2.0 * part * alpha * bv + alpha * alpha * vv)
    alpha_next = norm_next / curve
    on_source = alpha + alpha_next * (1.0 + beta)
    on_image = -alpha_next * alpha

    count = got.shape[0]
    code = got[:, :SLOTS].astype(jnp.int32)
    code_across = across[:SLOTS].astype(jnp.int32)
    terms = on_source * across[SLOTS : 2 * SLOTS] + on_image * across[2 * SLOTS : 3 * SLOTS]
    pieces = split3(terms)
    lane = lax.broadcasted_iota(jnp.int32, (count, LANES), 1)
    high = lax.broadcasted_iota(jnp.int32, (8 * tiles, count), 0)
    low_code = code & (LANES - 1)
    high_code = code_across >> 7
    for slot in range(SLOTS):
        span = pl.ds(slot * count, count)
        wide[span, :] = (lane == low_code[:, slot : slot + 1]).astype(jnp.float32).astype(jnp.bfloat16)
        here = high == high_code[slot : slot + 1, :]
        for index, piece in enumerate(pieces):
            tall[pl.ds(index * 8 * tiles, 8 * tiles), span] = jnp.where(
                here, piece[slot : slot + 1, :], 0.0
            ).astype(jnp.bfloat16)
    summed = jnp.dot(tall[...], wide[...], preferred_element_type=jnp.float32)
    summed = summed[: 8 * tiles] + summed[8 * tiles : 16 * tiles] + summed[16 * tiles :]
    loads = jnp.concatenate([summed[8 * t : 8 * t + 8] for t in range(tiles)], axis=1)
    fault_load = tectonic_ref[...] + loads[:patches]

    for x in range(0, source_ref.shape[0], 4):
        pressure[x : x + 4] = on_source[None] * source_ref[x : x + 4] + on_image[None] * image_ref[x : x + 4]

    leaving = pltpu.make_async_copy(pressure, pressure_ref, sem)
    leaving.start()

    piece_row = lax.broadcasted_iota(jnp.int32, (16, patches * LANES), 0)
    piece_lane = lax.broadcasted_iota(jnp.int32, (16, patches * LANES), 1)
    choose = onehot((piece_row & 3) == (piece_lane >> 7))

    def times_matrix(vector):
        pieces = jnp.concatenate([*split3(vector), jnp.zeros_like(vector)], axis=0)
        turned[...] = jnp.dot(
            pieces.T.astype(jnp.bfloat16), choose, preferred_element_type=jnp.float32
        )
        group = 16

        def body(i, sums):
            sums = list(sums)
            for g in range(group):
                start = pl.multiple_of(i * (8 * group), 8 * group) + 8 * g
                for p in range(patches):
                    spread = turned[pl.ds(start, 8), p * LANES : (p + 1) * LANES]
                    sums[p] = sums[p] + matrix_ref[p, pl.ds(start, 8), :] * jnp.concatenate(
                        [spread] * tiles, axis=1
                    )
            return tuple(sums)

        zero = jnp.zeros((8, unknowns), jnp.float32)
        sums = lax.fori_loop(0, unknowns // (8 * group), body, (zero,) * patches)
        for p in range(patches):
            rows[p : p + 1, :] = jnp.sum(sums[p], axis=0, keepdims=True)
        return rows[:patches, :]

    def mean(values):
        return jnp.sum(values, axis=1, keepdims=True) * (1.0 / unknowns)

    limit = yield_ref[...]
    row = lax.broadcasted_iota(jnp.int32, (patches, unknowns), 0)
    slip_now = None
    previous = None
    previous_image = None
    for iteration in range(steps):
        if iteration == 0:
            gradient = -fault_load
        else:
            gradient = times_matrix(slip_now) - fault_load
        free_part = jnp.where(free_ref[iteration] == 1, gradient, 0.0)
        kind = jnp.zeros((patches, unknowns), jnp.int32)
        for p in range(patches):
            kind = jnp.where(row == p, kind_ref[iteration, p], kind)
        conjugate = free_part
        if iteration > 0:
            conjugacy = mean(free_part * previous_image) / curved
            conjugate = free_part - conjugacy * previous
        direction = jnp.where(
            kind == 0, conjugate, jnp.where(kind == 1, gradient - free_part, gradient)
        )
        image_vec = times_matrix(direction)
        curved = mean(direction * image_vec) + 1e-06
        step_length = mean(gradient * direction) / curved
        moved = -step_length * direction if iteration == 0 else slip_now - step_length * direction
        slip_now = jnp.clip(moved, -limit, limit)
        previous = direction
        previous_image = image_vec
    slip_ref[...] = slip_now
    leaving.wait()


def finish(got, tectonic_load, yield_limit, free_mask, step_kind, patch_matrix, source, image):
    patches, unknowns = tectonic_load.shape
    tiles = unknowns // LANES
    count = got.shape[0]
    vmem = pl.BlockSpec(memory_space=pltpu.VMEM)
    return pl.pallas_call(
        functools.partial(final_kernel, step_kind.shape[0]),
        out_shape=(
            jax.ShapeDtypeStruct(source.shape, jnp.float32),
            jax.ShapeDtypeStruct(tectonic_load.shape, jnp.float32),
        ),
        in_specs=[pl.BlockSpec(memory_space=pltpu.SMEM)] + [vmem] * 7,
        out_specs=(pl.BlockSpec(memory_space=pl.ANY), vmem),
        scratch_shapes=[
            pltpu.VMEM(source.shape, jnp.float32),
            pltpu.VMEM((SLOTS * count, LANES), jnp.bfloat16),
            pltpu.VMEM((24 * tiles, SLOTS * count), jnp.bfloat16),
            pltpu.VMEM((unknowns, patches * LANES), jnp.float32),
            pltpu.VMEM((8, unknowns), jnp.float32),
            pltpu.SemaphoreType.DMA,
        ],
        compiler_params=pltpu.CompilerParams(vmem_limit_bytes=20 * 2**20),
        name="finish",
    )(step_kind, got, tectonic_load, yield_limit, free_mask, patch_matrix, source, image)


def is_even(axis):
    return (lax.axis_index(axis) + 1) % 2


WANTED = ((0, 0), (0, 1), (1, 0), (1, 1), (2, 0))


def edges_kernel(source_ref, perm_ref, storage_ref, first_ref, second_ref, sems):
    planes = source_ref.shape[0]
    fields = (source_ref, perm_ref, storage_ref)
    even = is_even("cell")
    copies = []
    for n, (f, deep) in enumerate(WANTED):
        for k, out in enumerate((first_ref, second_ref)):
            at_end = even if k == 0 else 1 - even
            plane = deep + at_end * (planes - 1 - 2 * deep)
            copies.append(pltpu.make_async_copy(fields[f].at[plane], out.at[n], sems.at[2 * n + k]))
    for copy in copies:
        copy.start()
    for copy in copies:
        copy.wait()


def edges(source, permeability, storage):
    vmem = pl.BlockSpec(memory_space=pltpu.VMEM)
    side = jax.ShapeDtypeStruct((5,) + source.shape[1:], jnp.float32)
    return pl.pallas_call(
        edges_kernel,
        out_shape=(side, side),
        in_specs=[pl.BlockSpec(memory_space=pl.ANY)] * 3,
        out_specs=(vmem,) * 2,
        scratch_shapes=[pltpu.SemaphoreType.DMA((10,))],
        compiler_params=pltpu.CompilerParams(vmem_limit_bytes=EDGES),
        name="edges",
    )(source, permeability, storage)


def corners_kernel(one_ref, two_ref, first_in_ref, second_in_ref, first_ref, second_ref):
    height = one_ref.shape[1]
    last = first_ref.shape[1] - 7
    even_cell = is_even("cell") == 1
    even_sub = is_even("sub")
    first_ref[...] = first_in_ref[...]
    second_ref[...] = second_in_ref[...]
    for k, out in enumerate((first_ref, second_ref)):
        at_end = even_sub if k == 0 else 1 - even_sub
        row = pl.ds(at_end * (height - 1), 1)
        for n in (0, 2):
            one, two = one_ref[n, row, :], two_ref[n, row, :]
            out[n, 0:1, :] = jnp.where(even_cell, two, one)
            out[n, last : last + 1, :] = jnp.where(even_cell, one, two)


def corners(cells, lines):
    vmem = pl.BlockSpec(memory_space=pltpu.VMEM)
    line = jax.ShapeDtypeStruct(lines[0].shape, jnp.float32)
    return pl.pallas_call(
        corners_kernel,
        out_shape=(line, line),
        in_specs=[vmem] * 4,
        out_specs=(vmem, vmem),
        compiler_params=pltpu.CompilerParams(vmem_limit_bytes=8 * 2**20),
        name="corners",
    )(*cells, *lines)


def swap_pairs(first_sent, second_sent, axis):
    count = lax.axis_size(axis)
    first = [(i, i ^ 1) for i in range(count)]
    second = [(i, i + 1) for i in range(1, count - 1, 2)]
    second = second + [(j, i) for i, j in second]
    return lax.ppermute(first_sent, axis, first), lax.ppermute(second_sent, axis, second)


def load_code(face_dof, unknowns):
    patch, unknown = face_dof // unknowns, face_dof % unknowns
    return ((unknown // LANES * 8 + patch) * LANES + unknown % LANES).astype(jnp.float32)


def on_device(
    source,
    permeability,
    storage,
    face_cell,
    face_dest,
    face_dof,
    face_weight,
    tectonic_load,
    patch_matrix,
    yield_limit,
    free_mask,
    step_kind,
):
    planes, height, depth = source.shape
    sides = edges(source, permeability, storage)
    cells = swap_pairs(*sides, "cell")
    *inner, first, second = image_inside(source, permeability, storage)
    lines = corners(cells, (first, second))
    subs = swap_pairs(*lines, "sub")

    where = (face_cell >> 7) % 2 * (planes * height) + (face_cell >> 8)
    dest = face_dest[:, 0]
    sent, slots, picker = faces(
        source, where, face_cell & (LANES - 1), dest, load_code(face_dof, tectonic_load.shape[1]), face_weight
    )
    image, sent = norms(
        where, dest, (slots, picker, sent), sides, cells, lines, subs, inner, source, storage
    )
    got = lax.all_to_all(sent, AXES, 0, 0, tiled=True)
    pressure_change, slip = finish(
        got, tectonic_load, yield_limit, free_mask, step_kind, patch_matrix, source, image
    )
    return (pressure_change, slip)


def solution(mesh):
    return jax.shard_map(
        on_device,
        mesh=mesh,
        in_specs=(
            P("cell", "sub", None),
            P("cell", "sub", None),
            P("cell", "sub", None),
            P(("cell", "sub")),
            P(("cell", "sub"), None),
            P(("cell", "sub")),
            P(("cell", "sub")),
            P(("cell", "sub"), None),
            P(("cell", "sub"), None, None),
            P(("cell", "sub"), None),
            P(None, ("cell", "sub"), None),
            P(None, ("cell", "sub")),
        ),
        out_specs=(P("cell", "sub", None), P(("cell", "sub"), None)),
        check_vma=False,
    )
```

time: 86.2 us -> 61.4 us (0.71)
  local copies, waits for them, and re-layouts: 13.5 us -> 0.07 us
  Pallas kernels: 37.1 us -> 29.1 us
  other arithmetic: 4.3 us -> 0.04 us
  blocking collectives: 19.7 us -> 23.2 us
  starting transfers between devices: 9.98 us -> 7.93 us
    unnamed x30 -> x26, local copies, waits for them, and re-layouts: 6.19 us -> 0.07 us
    slice x6 -> x0, local copies, waits for them, and re-layouts: 5.89 us -> none  [the longest x3 3.13 us: column(): array[:, y]]
    pallas_call x1, Pallas kernels: 10.2 us -> 5.17 us  [faces(): pl.pallas_call(faces_kernel, out_shape=(jax.ShapeDtypeStruct((LANES, LANE...]
    all_to_all x1, blocking collectives: 19.7 us -> 23.2 us  [on_device(): got = lax.all_to_all(sent, AXES, 0, 0, tiled=True)]
    unnamed x7 -> x0, other arithmetic: 2.15 us -> none
    pallas_call x1 -> x4, Pallas kernels: 14.7 us -> 12.7 us  [the longest x1 5.55 us: norms(): pl.pallas_call(norms_kernel, out_shape=(jax.ShapeDtypeStruct(source.shape...]
    ppermute x4, starting transfers between devices: 9.98 us -> 7.93 us  [the longest x2 4.63 us: swap_pairs(): lax.ppermute(second_sent, axis, second)]
    select_n x3 -> x0, other arithmetic: 2 us -> none  [the longest x1 1.13 us: on_device(): before = jnp.where(even_cell, cells[1], cells[0])]
  transfers between devices with their start and end apart: 4 -> 4, of which waited for: 0 -> 0; matrix products, arithmetic and copies ran while one was open for 7% -> 0% of each run, Pallas kernels for 12% -> 17%
where the time goes in v2:
time: 61.4 us; the launch traced here: 61.2 us
  Pallas kernels  29.1 us (47%)
  blocking collectives  23.2 us (38%)
  starting transfers between devices  7.93 us (13%)
  between operations  0.89 us (1%)
    all_to_all x1, blocking collectives, on_device(): got = lax.all_to_all(sent, AXES, 0, 0, tiled=True)  23.2 us
    pallas_call x1, Pallas kernels, finish(): pl.pallas_call(functools.partial(final_kernel, step_kind.shape[0]), out_s...  11.2 us
    pallas_call x1, Pallas kernels, norms(): pl.pallas_call(norms_kernel, out_shape=(jax.ShapeDtypeStruct(source.shape...  5.55 us
    pallas_call x1, Pallas kernels, faces(): pl.pallas_call(faces_kernel, out_shape=(jax.ShapeDtypeStruct((LANES, LANE...  5.17 us
    pallas_call x1, Pallas kernels, image_inside(): pl.pallas_call(image_kernel, out_shape=(block,) * 4 + (jax.ShapeDtypeStru...  5.08 us
    ppermute x2, starting transfers between devices, swap_pairs(): lax.ppermute(second_sent, axis, second)  4.63 us
    ppermute x2, starting transfers between devices, swap_pairs(): lax.ppermute(first_sent, axis, first)  3.29 us
    pallas_call x1, Pallas kernels, edges(): pl.pallas_call(edges_kernel, out_shape=(side, side), in_specs=[pl.BlockSp...  2 us
  transfers between devices with their start and end apart: 4, of which 0 were waited for; matrix products, arithmetic and copies ran while one was open for 0% of the time, Pallas kernels for 17%

profile of v2, /device:TPU:1, one launch (start us, length us, event | category | flops | bytes accessed | tf_op | source)
XLA Modules:
  0.0 61.2 jit_solution(17443879364527534887)
XLA Ops:
  0.6 0.0 copy-start
  0.6 2.0 %edges.1 = (f32[5,48,256]{2,1,0:T(8,128)}, f32[5,48,256]{2,1,0:T(8,128)}) custom-call(f32[32,48,256]{2,1,0:T(8,128)} %source_ref.7, f32[32,48,256]{2,1,0:T(8,128)} %perm_ref.3, f32[32,48,256]{2,1,0:T(8,128)} %storage_ref.5), custom_call_target="tpu_custom_call" | custom-call | tf_op jit(solution)/shard_map/edges/pallas_call | solution.py:702
  2.6 2.1 %collective-permute-start = (f32[5,48,256]{2,1,0:T(8,128)}, f32[5,48,256]{2,1,0:T(8,128)S(1)}, u32[]{:S(2)}, u32[]{:S(2)}) collective-permute-start(f32[5,48,256]{2,1,0:T(8,128)} %get-tuple-element.21.side_first_ref), channel_id=1, source_target_pairs={{0,8},{8,0},{16,24},{24,16},{32,40},{40,32},{48,56},{56,48},{64,72... | collective-permute-start | bytes 737288 | tf_op jit(solution)/shard_map/ppermute | solution.py:747
  4.8 0.8 %collective-permute-start.1 = (f32[5,48,256]{2,1,0:T(8,128)}, f32[5,48,256]{2,1,0:T(8,128)S(1)}, u32[]{:S(2)}, u32[]{:S(2)}) collective-permute-start(f32[5,48,256]{2,1,0:T(8,128)} %get-tuple-element.22.side_second_ref), channel_id=1, source_target_pairs={{8,16},{24,32},{40,48},{56,64},{72,80},{88,96},{104,112},{16,8},{3... | collective-permute-start | bytes 737288 | tf_op jit(solution)/shard_map/ppermute | solution.py:747
  5.6 5.1 %image.1 = (f32[32,48,256]{2,1,0:T(8,128)S(1)}, f32[32,48,256]{2,1,0:T(8,128)S(1)}, f32[32,48,256]{2,1,0:T(8,128)S(1)}, f32[32,48,256]{2,1,0:T(8,128)S(1)}, f32[...) custom-call(f32[32,48,256]{2,1,0:T(8,128)S(1)} %copy-done, f32[32,48,256]{2,1,0:T(8,128)} %perm_ref.3, ...), custom_call_target="tpu_custom_call" | custom-call | tf_op jit(solution)/shard_map/image/pallas_call | solution.py:276
  10.7 0.0 copy-start.1
  10.7 0.0 copy-start.3
  10.7 0.0 copy-start.4
  10.8 0.0 collective-permute-done.one_ref.cell_first_ref
  10.8 0.0 collective-permute-done.1.two_ref.cell_second_ref
  10.8 1.2 %collective-permute-start.2 = (f32[5,40,256]{2,1,0:T(8,128)S(1)}, f32[5,40,256]{2,1,0:T(8,128)S(1)}, u32[]{:S(2)}, u32[]{:S(2)}) collective-permute-start(f32[5,40,256]{2,1,0:T(8,128)S(1)} %get-tuple-element.25.line_first_ref), channel_id=1, source_target_pairs={{0,1},{1,0},{2,3},{3,2},{4,5},{5,4},{6,7},{7,6},{8,9},{9,8},{10,11... | collective-permute-start | bytes 614408 | tf_op jit(solution)/shard_map/ppermute | solution.py:747
  12.0 3.8 %collective-permute-start.3 = (f32[5,40,256]{2,1,0:T(8,128)S(1)}, f32[5,40,256]{2,1,0:T(8,128)S(1)}, u32[]{:S(2)}, u32[]{:S(2)}) collective-permute-start(f32[5,40,256]{2,1,0:T(8,128)S(1)} %get-tuple-element.26.line_second_ref), channel_id=1, source_target_pairs={{1,2},{3,4},{5,6},{2,1},{4,3},{6,5},{9,10},{11,12},{13,14},{10,9},... | collective-permute-start | bytes 614408 | tf_op jit(solution)/shard_map/ppermute | solution.py:747
  15.8 0.0 copy-done.11
  15.9 5.2 %faces.1 = (f32[128,128]{1,0:T(8,128)S(1)}, bf16[128,2048]{1,0:T(8,128)(2,1)S(1)}, f32[128,2048]{1,0:T(8,128)S(1)}) custom-call(s32[2048]{0:T(1024)S(1)} %get-tuple-element.35.where_ref, s32[16,128]{1,0:T(8,128)S(1)} %bitcast.14, f32[16,128]{1,0:T(8,128)S(1)} %fusion.8.code_ref, f32[16,128]{1,0:T(8,128)S(1)} %bitcast.16, ...), custom_call_target="tpu_custom_call" | custom-call | tf_op jit(solution)/shard_map/faces/pallas_call | solution.py:140
  21.1 0.0 collective-permute-done.2.sub_first_ref
  21.1 0.0 collective-permute-done.3.sub_second_ref
  21.1 0.0 copy-start.2
  21.1 0.0 copy-start.5
  21.1 0.0 copy-start.7
  21.2 0.0 copy-start.8
  21.2 0.0 copy-start.10
  21.2 5.5 %norms.1 = (f32[32,48,256]{2,1,0:T(8,128)S(1)}, f32[128,128]{1,0:T(8,128)S(1)}) custom-call(s32[2048]{0:T(1024)S(1)} %get-tuple-element.35.where_ref, s32[16,128]{1,0:T(8,128)S(1)} %bitcast.15, bf16[128,2048]{1,0:T(8,128)(2,1)S(1)} %get-tuple-element.18.slots_ref, f32[128,2048]{1,0:T(8,128)S(1)} %get-tuple-element.19.picker_ref, ...), custom_call_target="tpu_custom_call" | custom-call | tf_op jit(solution)/shard_map/norms/pallas_call | solution.py:496
  26.7 23.2 %all_to_all.11 = f32[128,1,128]{2,1,0:T(1,128)S(1)} all-to-all(f32[128,1,128]{2,1,0:T(1,128)S(1)} %bitcast.13), channel_id=1, replica_groups=mesh['cell'=16,'sub'=8] {'cell','sub'}, dimensions={0} | all-to-all | bytes 131072 | tf_op jit(solution)/shard_map/all_to_all | solution.py:784
  49.9 11.2 %finish.1 = (f32[32,48,256]{2,1,0:T(8,128)}, f32[4,768]{1,0:T(4,128)}) custom-call(s32[4,4]{1,0:T(4,128)S(1)} %copy-done.10, f32[128,128]{1,0:T(8,128)S(1)} %bitcast.12, f32[4,768]{1,0:T(4,128)S(1)} %copy-done.7, f32[4,768]{1,0:T(4,128)S(1)} %copy-done.8, s32[4,4,768]{2,1,0:T(4,128)S(1)} %copy-done.5, f32[4,768,768]{2,1,0:T(8,128)S(1)} %copy-done.2, ...), custom_call_target="tpu_custom_call" | custom-call | tf_op jit(solution)/shard_map/finish/pallas_call | solution.py:655
  (19 shorter events, 0.1 us)
Async XLA Ops:
  0.6 5.0 %copy-start = (f32[32,48,256]{2,1,0:T(8,128)S(1)}, f32[32,48,256]{2,1,0:T(8,128)}, u32[]{:S(2)}) copy-start(f32[32,48,256]{2,1,0:T(8,128)} %source_ref.7) | copy-start | bytes 4718596
  2.6 8.1 %collective-permute-start = (f32[5,48,256]{2,1,0:T(8,128)}, f32[5,48,256]{2,1,0:T(8,128)S(1)}, u32[]{:S(2)}, u32[]{:S(2)}) collective-permute-start(f32[5,48,256]{2,1,0:T(8,128)} %get-tuple-element.21.side_first_ref), channel_id=1, source_target_pairs={{0,8},{8,0},{16,24},{24,16},{32,40},{40,32},{48,56},{56,48},{64,72... | collective-permute-start | bytes 737288 | tf_op jit(solution)/shard_map/ppermute | solution.py:747
  4.8 5.9 %copy-start.12 = (s32[2048]{0:T(1024)S(1)}, s32[2048]{0:T(1024)}, u32[]{:S(2)}) copy-start(s32[2048]{0:T(1024)} %param.17) | copy-start | bytes 24580
  4.8 11.1 %copy-start.11 = (s32[2048]{0:T(1024)S(1)}, s32[2048]{0:T(1024)}, u32[]{:S(2)}) copy-start(s32[2048]{0:T(1024)} %param.15) | copy-start | bytes 24580
  4.8 11.1 %copy-start.6 = (s32[2048,1]{0,1:T(1,128)S(1)}, s32[2048,1]{0,1:T(1,128)}, u32[]{:S(2)}) copy-start(s32[2048,1]{0,1:T(1,128)} %param.16) | copy-start | bytes 24580
  4.8 11.1 %copy-start.9 = (f32[2048]{0:T(1024)S(1)}, f32[2048]{0:T(1024)}, u32[]{:S(2)}) copy-start(f32[2048]{0:T(1024)} %param.18) | copy-start | bytes 24580
  4.8 6.0 %collective-permute-start.1 = (f32[5,48,256]{2,1,0:T(8,128)}, f32[5,48,256]{2,1,0:T(8,128)S(1)}, u32[]{:S(2)}, u32[]{:S(2)}) collective-permute-start(f32[5,48,256]{2,1,0:T(8,128)} %get-tuple-element.22.side_second_ref), channel_id=1, source_target_pairs={{8,16},{24,32},{40,48},{56,64},{72,80},{88,96},{104,112},{16,8},{3... | collective-permute-start | bytes 737288 | tf_op jit(solution)/shard_map/ppermute | solution.py:747
  10.7 10.4 %copy-start.1 = (f32[32,48,256]{2,1,0:T(8,128)S(1)}, f32[32,48,256]{2,1,0:T(8,128)}, u32[]{:S(2)}) copy-start(f32[32,48,256]{2,1,0:T(8,128)} %storage_ref.5) | copy-start | bytes 4718596
  10.7 10.4 %copy-start.3 = (f32[5,48,256]{2,1,0:T(8,128)S(1)}, f32[5,48,256]{2,1,0:T(8,128)}, u32[]{:S(2)}) copy-start(f32[5,48,256]{2,1,0:T(8,128)} %get-tuple-element.21.side_first_ref) | copy-start | bytes 737284
  10.7 10.4 %copy-start.4 = (f32[5,48,256]{2,1,0:T(8,128)S(1)}, f32[5,48,256]{2,1,0:T(8,128)}, u32[]{:S(2)}) copy-start(f32[5,48,256]{2,1,0:T(8,128)} %get-tuple-element.22.side_second_ref) | copy-start | bytes 737284
  10.8 10.2 %collective-permute-start.2 = (f32[5,40,256]{2,1,0:T(8,128)S(1)}, f32[5,40,256]{2,1,0:T(8,128)S(1)}, u32[]{:S(2)}, u32[]{:S(2)}) collective-permute-start(f32[5,40,256]{2,1,0:T(8,128)S(1)} %get-tuple-element.25.line_first_ref), channel_id=1, source_target_pairs={{0,1},{1,0},{2,3},{3,2},{4,5},{5,4},{6,7},{7,6},{8,9},{9,8},{10,11... | collective-permute-start | bytes 614408 | tf_op jit(solution)/shard_map/ppermute | solution.py:747
  12.0 9.1 %collective-permute-start.3 = (f32[5,40,256]{2,1,0:T(8,128)S(1)}, f32[5,40,256]{2,1,0:T(8,128)S(1)}, u32[]{:S(2)}, u32[]{:S(2)}) collective-permute-start(f32[5,40,256]{2,1,0:T(8,128)S(1)} %get-tuple-element.26.line_second_ref), channel_id=1, source_target_pairs={{1,2},{3,4},{5,6},{2,1},{4,3},{6,5},{9,10},{11,12},{13,14},{10,9},... | collective-permute-start | bytes 614408 | tf_op jit(solution)/shard_map/ppermute | solution.py:747
  21.1 28.8 %copy-start.2 = (f32[4,768,768]{2,1,0:T(8,128)S(1)}, f32[4,768,768]{2,1,0:T(8,128)}, u32[]{:S(2)}) copy-start(f32[4,768,768]{2,1,0:T(8,128)} %matrix_ref.1) | copy-start | bytes 28311556
  21.1 28.8 %copy-start.5 = (s32[4,4,768]{2,1,0:T(4,128)S(1)}, s32[4,4,768]{2,1,0:T(4,128)}, u32[]{:S(2)}) copy-start(s32[4,4,768]{2,1,0:T(4,128)} %free_ref.1) | copy-start | bytes 147460
  21.1 28.8 %copy-start.7 = (f32[4,768]{1,0:T(4,128)S(1)}, f32[4,768]{1,0:T(4,128)}, u32[]{:S(2)}) copy-start(f32[4,768]{1,0:T(4,128)} %tectonic_ref.1) | copy-start | bytes 36868
  21.2 28.8 %copy-start.8 = (f32[4,768]{1,0:T(4,128)S(1)}, f32[4,768]{1,0:T(4,128)}, u32[]{:S(2)}) copy-start(f32[4,768]{1,0:T(4,128)} %yield_ref.1) | copy-start | bytes 36868
  21.2 28.8 %copy-start.10 = (s32[4,4]{1,0:T(4,128)S(1)}, s32[4,4]{1,0:T(4,128)}, u32[]{:S(2)}) copy-start(s32[4,4]{1,0:T(4,128)} %kind_ref.1) | copy-start | bytes 196

commit v3 on v2

--- a/solution.py
+++ b/solution.py
@@ -64,8 +64,7 @@
         picks[pl.ds(first + j, 1), :] = table[pl.ds(where_ref[first + j], 1), :]
 
 
-def faces_kernel(
-    where_ref,
+def slots_kernel(
     dest_ref,
     code_ref,
     weight_ref,
@@ -74,8 +73,7 @@
     sent_ref,
     slots_ref,
     picker_ref,
-    table,
-    picks,
+    table_ref,
     owners,
     spread,
     sems,
@@ -84,7 +82,7 @@
     rows = source_ref.shape[0]
     halves = [
         pltpu.make_async_copy(
-            source_ref.at[:, pl.ds(t * LANES, LANES)], table.at[pl.ds(t * rows, rows), :], sems.at[t]
+            source_ref.at[:, pl.ds(t * LANES, LANES)], table_ref.at[pl.ds(t * rows, rows), :], sems.at[t]
         )
         for t in range(2)
     ]
@@ -114,48 +112,78 @@
         slots_ref[:, span] = slots.astype(jnp.bfloat16)
         picker_ref[:, span] = jnp.where(lane_number == lane_spread[:, cut], weight_spread[:, cut], 0.0)
         owners[:, span] = onehot(row_number == dest[c : c + 1, :])
-        spread[span, :LANES] = grouped_pieces(code_spread[:, cut], slots)
+        spread[span, :] = grouped_pieces(code_spread[:, cut], slots)
+    sent_ref[...] = join_groups(dot(owners[...], spread[...]), 0)
     for half in halves:
         half.wait()
 
+
+def values_kernel(
+    where_ref, dest_ref, slots_ref, picker_ref, sent_in_ref, table_ref, sent_ref, picks, owners, spread
+):
+    chunks = dest_ref.shape[0]
+
     def gather(i, carry):
-        copy_rows(table, picks, where_ref, i * 64, 64)
+        copy_rows(table_ref, picks, where_ref, i * 64, 64)
         return carry
 
     lax.fori_loop(0, chunks * LANES // 64, gather, 0)
-    for c in range(chunks):
+    face_values(dest_ref, slots_ref, picker_ref, picks, owners, spread)
+    sent_ref[...] = sent_in_ref[...] + join_groups(dot(owners[...], spread[...]), 1)
+
+
+def face_values(dest_ref, slots_ref, picker_ref, picks, owners, spread):
+    dest = dest_ref[...]
+    owner = lax.broadcasted_iota(jnp.int32, (LANES, LANES), 0)
+    for c in range(dest.shape[0]):
         span = pl.ds(c * LANES, LANES)
+        owners[:, span] = onehot(owner == dest[c : c + 1, :])
         value = sum_lanes(picks[span, :] * picker_ref[:, span])
-        spread[span, LANES:] = grouped_pieces(value, slots_ref[:, span].astype(jnp.float32))
-    summed = dot(owners[...], spread[...])
-    sent_ref[...] = join_groups(summed[:, :LANES], 0) + join_groups(summed[:, LANES:], 1)
-
-
-def faces(source, where, lane, dest, code, weight):
-    count = where.shape[0]
+        spread[span, :] = grouped_pieces(value, slots_ref[:, span].astype(jnp.float32))
+
+
+def face_slots(source, lane, dest, code, weight):
+    count = dest.shape[0]
     chunks = count // LANES
     rows = source.shape[0] * source.shape[1]
     vmem = pl.BlockSpec(memory_space=pltpu.VMEM)
     cut = lambda values: values.reshape(chunks, LANES)
     return pl.pallas_call(
-        faces_kernel,
+        slots_kernel,
         out_shape=(
             jax.ShapeDtypeStruct((LANES, LANES), jnp.float32),
             jax.ShapeDtypeStruct((LANES, count), jnp.bfloat16),
             jax.ShapeDtypeStruct((LANES, count), jnp.float32),
+            jax.ShapeDtypeStruct((2 * rows, LANES), jnp.float32),
         ),
-        in_specs=[pl.BlockSpec(memory_space=pltpu.SMEM)] + [vmem] * 4 + [pl.BlockSpec(memory_space=pltpu.HBM)],
-        out_specs=(vmem, vmem, vmem),
+        in_specs=[vmem] * 4 + [pl.BlockSpec(memory_space=pl.ANY)],
+        out_specs=(vmem,) * 4,
         scratch_shapes=[
-            pltpu.VMEM((2 * rows, LANES), jnp.float32),
+            pltpu.VMEM((LANES, count), jnp.bfloat16),
+            pltpu.VMEM((count, LANES), jnp.bfloat16),
+            pltpu.SemaphoreType.DMA((2,)),
+        ],
+        compiler_params=pltpu.CompilerParams(vmem_limit_bytes=8 * 2**20),
+        name="slots",
+    )(cut(dest), cut(code), cut(weight), cut(lane), source.reshape(rows, source.shape[2]))
+
+
+def add_values(where, dest, slots, picker, sent, table):
+    count = where.shape[0]
+    vmem = pl.BlockSpec(memory_space=pltpu.VMEM)
+    return pl.pallas_call(
+        values_kernel,
+        out_shape=jax.ShapeDtypeStruct((LANES, LANES), jnp.float32),
+        in_specs=[pl.BlockSpec(memory_space=pltpu.SMEM)] + [vmem] * 5,
+        out_specs=vmem,
+        scratch_shapes=[
             pltpu.VMEM((count, LANES), jnp.float32),
             pltpu.VMEM((LANES, count), jnp.bfloat16),
-            pltpu.VMEM((count, 2 * LANES), jnp.bfloat16),
-            pltpu.SemaphoreType.DMA((2,)),
+            pltpu.VMEM((count, LANES), jnp.bfloat16),
         ],
-        compiler_params=pltpu.CompilerParams(vmem_limit_bytes=12 * 2**20),
-        name="faces",
-    )(where, cut(dest), cut(code), cut(weight), cut(lane), source.reshape(rows, source.shape[2]))
+        compiler_params=pltpu.CompilerParams(vmem_limit_bytes=8 * 2**20),
+        name="values",
+    )(where, dest.reshape(count // LANES, LANES), slots, picker, sent, table)
 
 
 def image_kernel(
@@ -433,7 +461,7 @@
         complete(x, None)
         return carry
 
-    lax.fori_loop(1, planes - 1, middle, 0)
+    lax.fori_loop(0, planes // 2 - 1, lambda n, c: middle(2 * n + 2, middle(2 * n + 1, c)), 0)
     complete(planes - 1, flow_hi)
     v_hi = w_hi - mu * b_hi
     vy_hi = wy_hi - mu * by_hi
@@ -461,7 +489,8 @@
         return vv, vav
 
     zero = jnp.zeros((8, depth), jnp.float32)
-    vv, vav = [total(values) for values in lax.fori_loop(0, planes, measure, (zero, zero))]
+    sums = lax.fori_loop(0, planes // 2, lambda n, s: measure(2 * n + 1, measure(2 * n, s)), (zero, zero))
+    vv, vav = [total(values) for values in sums]
     v_head, v_tail = rest[0], rest[planes - 1]
     vy_head, vy_tail = lines[0], lines[1]
     bv = vv - total(flow_hi * v_hi) - rows_total(flowy_hi * vy_hi)
@@ -469,14 +498,7 @@
     vav = vav + total(con_hi * ((v_tail - v_hi) * (v_tail - v_hi)))
     vav = vav + rows_total(cony_hi * ((vy_tail - vy_hi) * (vy_tail - vy_hi)))
 
-    chunks = dest_ref.shape[0]
-    dest = dest_ref[...]
-    owner = lax.broadcasted_iota(jnp.int32, (LANES, LANES), 0)
-    for c in range(chunks):
-        span = pl.ds(c * LANES, LANES)
-        owners[:, span] = onehot(owner == dest[c : c + 1, :])
-        value = sum_lanes(picks[span, :] * picker_ref[:, span])
-        spread[span, :] = grouped_pieces(value, slots_ref[:, span].astype(jnp.float32))
+    face_values(dest_ref, slots_ref, picker_ref, picks, owners, spread)
     summed = dot(owners[...], spread[...])
     sent = sent_in_ref[...] + join_groups(summed, 2)
     place = lax.broadcasted_iota(jnp.int32, sent.shape, 1)
@@ -510,7 +532,7 @@
             pltpu.VMEM((LANES, count), jnp.bfloat16),
             pltpu.VMEM((count, LANES), jnp.bfloat16),
         ],
-        compiler_params=pltpu.CompilerParams(vmem_limit_bytes=16 * 2**20),
+        compiler_params=pltpu.CompilerParams(vmem_limit_bytes=12 * 2**20),
         name="norms",
     )(where, *operands)
 
@@ -710,7 +732,7 @@
     )(source, permeability, storage)
 
 
-def corners_kernel(one_ref, two_ref, first_in_ref, second_in_ref, first_ref, second_ref):
+def corners_kernel(one_ref, two_ref, first_in_ref, second_in_ref, after_ref, first_ref, second_ref):
     height = one_ref.shape[1]
     last = first_ref.shape[1] - 7
     even_cell = is_even("cell") == 1
@@ -726,17 +748,17 @@
             out[n, last : last + 1, :] = jnp.where(even_cell, one, two)
 
 
-def corners(cells, lines):
+def corners(cells, lines, after):
     vmem = pl.BlockSpec(memory_space=pltpu.VMEM)
     line = jax.ShapeDtypeStruct(lines[0].shape, jnp.float32)
     return pl.pallas_call(
         corners_kernel,
         out_shape=(line, line),
-        in_specs=[vmem] * 4,
+        in_specs=[vmem] * 4 + [pl.BlockSpec(memory_space=pl.ANY)],
         out_specs=(vmem, vmem),
         compiler_params=pltpu.CompilerParams(vmem_limit_bytes=8 * 2**20),
         name="corners",
-    )(*cells, *lines)
+    )(*cells, *lines, after)
 
 
 def swap_pairs(first_sent, second_sent, axis):
@@ -770,14 +792,14 @@
     sides = edges(source, permeability, storage)
     cells = swap_pairs(*sides, "cell")
     *inner, first, second = image_inside(source, permeability, storage)
-    lines = corners(cells, (first, second))
+    dest = face_dest[:, 0]
+    sent, slots, picker, table = face_slots(
+        source, face_cell & (LANES - 1), dest, load_code(face_dof, tectonic_load.shape[1]), face_weight
+    )
+    lines = corners(cells, (first, second), sent)
     subs = swap_pairs(*lines, "sub")
-
     where = (face_cell >> 7) % 2 * (planes * height) + (face_cell >> 8)
-    dest = face_dest[:, 0]
-    sent, slots, picker = faces(
-        source, where, face_cell & (LANES - 1), dest, load_code(face_dof, tectonic_load.shape[1]), face_weight
-    )
+    sent = add_values(where, dest, slots, picker, sent, table)
     image, sent = norms(
         where, dest, (slots, picker, sent), sides, cells, lines, subs, inner, source, storage
     )

time: 61.4 us -> 59.5 us (0.969)
  blocking collectives: 23.2 us -> 21.9 us
  starting transfers between devices: 7.93 us -> 7.27 us
    all_to_all x1, blocking collectives: 23.2 us -> 21.9 us  [on_device(): got = lax.all_to_all(sent, AXES, 0, 0, tiled=True)]
    pallas_call x1 -> x2, Pallas kernels: 5.17 us -> 5.63 us  [the longest x1 3.69 us: add_values(): pl.pallas_call(values_kernel, out_shape=jax.ShapeDtypeStruct((LANES, LANE...]
  transfers between devices with their start and end apart: 4 -> 4, of which waited for: 0 -> 0; matrix products, arithmetic and copies ran while one was open for 0% -> 0% of each run, Pallas kernels for 17% -> 18%
where the time goes in v3:
time: 59.5 us; the launch traced here: 59.3 us
  Pallas kernels  29.1 us (49%)
  blocking collectives  21.9 us (37%)
  starting transfers between devices  7.27 us (12%)
  between operations  0.92 us (2%)
    all_to_all x1, blocking collectives, on_device(): got = lax.all_to_all(sent, AXES, 0, 0, tiled=True)  21.9 us
    pallas_call x1, Pallas kernels, finish(): pl.pallas_call(functools.partial(final_kernel, step_kind.shape[0]), out_s...  11.2 us
    pallas_call x1, Pallas kernels, norms(): pl.pallas_call(norms_kernel, out_shape=(jax.ShapeDtypeStruct(source.shape...  5.1 us
    pallas_call x1, Pallas kernels, image_inside(): pl.pallas_call(image_kernel, out_shape=(block,) * 4 + (jax.ShapeDtypeStru...  5.08 us
    ppermute x2, starting transfers between devices, swap_pairs(): lax.ppermute(second_sent, axis, second)  4.11 us
    pallas_call x1, Pallas kernels, add_values(): pl.pallas_call(values_kernel, out_shape=jax.ShapeDtypeStruct((LANES, LANE...  3.69 us
    ppermute x2, starting transfers between devices, swap_pairs(): lax.ppermute(first_sent, axis, first)  3.17 us
    pallas_call x1, Pallas kernels, edges(): pl.pallas_call(edges_kernel, out_shape=(side, side), in_specs=[pl.BlockSp...  2 us
  transfers between devices with their start and end apart: 4, of which 0 were waited for; matrix products, arithmetic and copies ran while one was open for 0% of the time, Pallas kernels for 18%

profile of v3, /device:TPU:1, one launch (start us, length us, event | category | flops | bytes accessed | tf_op | source)
XLA Modules:
  0.0 59.3 jit_solution(1860879450692916174)
XLA Ops:
  0.6 2.0 %edges.1 = (f32[5,48,256]{2,1,0:T(8,128)}, f32[5,48,256]{2,1,0:T(8,128)}) custom-call(f32[32,48,256]{2,1,0:T(8,128)} %source_ref.7, f32[32,48,256]{2,1,0:T(8,128)} %perm_ref.3, f32[32,48,256]{2,1,0:T(8,128)} %storage_ref.5), custom_call_target="tpu_custom_call" | custom-call | tf_op jit(solution)/shard_map/edges/pallas_call | solution.py:724
  2.7 2.1 %collective-permute-start = (f32[5,48,256]{2,1,0:T(8,128)}, f32[5,48,256]{2,1,0:T(8,128)S(1)}, u32[]{:S(2)}, u32[]{:S(2)}) collective-permute-start(f32[5,48,256]{2,1,0:T(8,128)} %get-tuple-element.23.side_first_ref), channel_id=1, source_target_pairs={{0,8},{8,0},{16,24},{24,16},{32,40},{40,32},{48,56},{56,48},{64,72... | collective-permute-start | bytes 737288 | tf_op jit(solution)/shard_map/ppermute | solution.py:769
  4.8 0.7 %collective-permute-start.1 = (f32[5,48,256]{2,1,0:T(8,128)}, f32[5,48,256]{2,1,0:T(8,128)S(1)}, u32[]{:S(2)}, u32[]{:S(2)}) collective-permute-start(f32[5,48,256]{2,1,0:T(8,128)} %get-tuple-element.24.side_second_ref), channel_id=1, source_target_pairs={{8,16},{24,32},{40,48},{56,64},{72,80},{88,96},{104,112},{16,8},{3... | collective-permute-start | bytes 737288 | tf_op jit(solution)/shard_map/ppermute | solution.py:769
  5.5 0.0 copy-start.11
  5.5 0.0 copy-start.5
  5.5 0.0 copy-start.9
  5.5 5.1 %image.1 = (f32[32,48,256]{2,1,0:T(8,128)S(1)}, f32[32,48,256]{2,1,0:T(8,128)S(1)}, f32[32,48,256]{2,1,0:T(8,128)S(1)}, f32[32,48,256]{2,1,0:T(8,128)S(1)}, f32[...) custom-call(f32[32,48,256]{2,1,0:T(8,128)S(1)} %copy-done, f32[32,48,256]{2,1,0:T(8,128)} %perm_ref.3, ...), custom_call_target="tpu_custom_call" | custom-call | tf_op jit(solution)/shard_map/image/pallas_call | solution.py:304
  10.7 1.9 %slots.1 = (f32[128,128]{1,0:T(8,128)S(1)}, bf16[128,2048]{1,0:T(8,128)(2,1)S(1)}, f32[128,2048]{1,0:T(8,128)S(1)}, f32[3072,128]{1,0:T(8,128)S(1)}) custom-call(s32[16,128]{1,0:T(8,128)S(1)} %bitcast.13, f32[16,128]{1,0:T(8,128)S(1)} %fusion.8.code_ref, f32[16,128]{1,0:T(8,128)S(1)} %bitcast.17, s32[16,128]{1,0:T(8,128)S(1)} %get-tuple-element.36.lane_ref, ...), custom_call_target="tpu_custom_call" | custom-call | tf_op jit(solution)/shard_map/slots/pallas_call | solution.py:151
  12.6 0.0 collective-permute-done.one_ref.cell_first_ref
  12.6 0.0 collective-permute-done.1.two_ref.cell_second_ref
  12.7 1.0 %collective-permute-start.2 = (f32[5,40,256]{2,1,0:T(8,128)S(1)}, f32[5,40,256]{2,1,0:T(8,128)S(1)}, u32[]{:S(2)}, u32[]{:S(2)}) collective-permute-start(f32[5,40,256]{2,1,0:T(8,128)S(1)} %get-tuple-element.27.line_first_ref), channel_id=1, source_target_pairs={{0,1},{1,0},{2,3},{3,2},{4,5},{5,4},{6,7},{7,6},{8,9},{9,8},{10,11... | collective-permute-start | bytes 614408 | tf_op jit(solution)/shard_map/ppermute | solution.py:769
  13.7 3.4 %collective-permute-start.3 = (f32[5,40,256]{2,1,0:T(8,128)S(1)}, f32[5,40,256]{2,1,0:T(8,128)S(1)}, u32[]{:S(2)}, u32[]{:S(2)}) collective-permute-start(f32[5,40,256]{2,1,0:T(8,128)S(1)} %get-tuple-element.28.line_second_ref), channel_id=1, source_target_pairs={{1,2},{3,4},{5,6},{2,1},{4,3},{6,5},{9,10},{11,12},{13,14},{10,9},... | collective-permute-start | bytes 614408 | tf_op jit(solution)/shard_map/ppermute | solution.py:769
  17.2 0.0 copy-start.1
  17.2 0.0 copy-start.3
  17.2 3.7 %values.1.sent_in_ref = f32[128,128]{1,0:T(8,128)S(1)} custom-call(s32[2048]{0:T(1024)S(1)} %get-tuple-element.37.where_ref, s32[16,128]{1,0:T(8,128)S(1)} %bitcast.14, bf16[128,2048]{1,0:T(8,128)(2,1)S(1)} %get-tuple-element.19.slots_ref, f32[128,2048]{1,0:T(8,128)S(1)} %get-tuple-element.20.picker_ref, ...), custom_call_target="tpu_custom_call" | custom-call | tf_op jit(solution)/shard_map/values/pallas_call | solution.py:174
  20.9 0.0 collective-permute-done.2.sub_first_ref
  21.0 0.0 copy-start.2
  21.0 0.0 copy-start.6
  21.0 0.0 copy-start.7
  21.0 0.0 copy-start.8
  21.0 0.0 copy-start.10
  21.0 5.1 %norms.1 = (f32[32,48,256]{2,1,0:T(8,128)S(1)}, f32[128,128]{1,0:T(8,128)S(1)}) custom-call(s32[2048]{0:T(1024)S(1)} %get-tuple-element.37.where_ref, s32[16,128]{1,0:T(8,128)S(1)} %bitcast.15, bf16[128,2048]{1,0:T(8,128)(2,1)S(1)} %get-tuple-element.19.slots_ref, f32[128,2048]{1,0:T(8,128)S(1)} %get-tuple-element.20.picker_ref, ...), custom_call_target="tpu_custom_call" | custom-call | tf_op jit(solution)/shard_map/norms/pallas_call | solution.py:518
  26.1 21.9 %all_to_all.11 = f32[128,1,128]{2,1,0:T(1,128)S(1)} all-to-all(f32[128,1,128]{2,1,0:T(1,128)S(1)} %bitcast.16), channel_id=1, replica_groups=mesh['cell'=16,'sub'=8] {'cell','sub'}, dimensions={0} | all-to-all | bytes 131072 | tf_op jit(solution)/shard_map/all_to_all | solution.py:806
  48.0 11.2 %finish.1 = (f32[32,48,256]{2,1,0:T(8,128)}, f32[4,768]{1,0:T(4,128)}) custom-call(s32[4,4]{1,0:T(4,128)S(1)} %copy-done.10, f32[128,128]{1,0:T(8,128)S(1)} %bitcast.12, f32[4,768]{1,0:T(4,128)S(1)} %copy-done.7, f32[4,768]{1,0:T(4,128)S(1)} %copy-done.8, s32[4,4,768]{2,1,0:T(4,128)S(1)} %copy-done.6, f32[4,768,768]{2,1,0:T(8,128)S(1)} %copy-done.2, ...), custom_call_target="tpu_custom_call" | custom-call | tf_op jit(solution)/shard_map/finish/pallas_call | solution.py:677
  (20 shorter events, 0.1 us)
Async XLA Ops:
  0.6 4.9 %copy-start = (f32[32,48,256]{2,1,0:T(8,128)S(1)}, f32[32,48,256]{2,1,0:T(8,128)}, u32[]{:S(2)}) copy-start(f32[32,48,256]{2,1,0:T(8,128)} %source_ref.7) | copy-start | bytes 4718596
  0.6 4.8 %copy-start.12 = (s32[2048]{0:T(1024)S(1)}, s32[2048]{0:T(1024)}, u32[]{:S(2)}) copy-start(s32[2048]{0:T(1024)} %param.17) | copy-start | bytes 24580
  2.7 10.0 %collective-permute-start = (f32[5,48,256]{2,1,0:T(8,128)}, f32[5,48,256]{2,1,0:T(8,128)S(1)}, u32[]{:S(2)}, u32[]{:S(2)}) collective-permute-start(f32[5,48,256]{2,1,0:T(8,128)} %get-tuple-element.23.side_first_ref), channel_id=1, source_target_pairs={{0,8},{8,0},{16,24},{24,16},{32,40},{40,32},{48,56},{56,48},{64,72... | collective-permute-start | bytes 737288 | tf_op jit(solution)/shard_map/ppermute | solution.py:769
  4.8 7.9 %collective-permute-start.1 = (f32[5,48,256]{2,1,0:T(8,128)}, f32[5,48,256]{2,1,0:T(8,128)S(1)}, u32[]{:S(2)}, u32[]{:S(2)}) collective-permute-start(f32[5,48,256]{2,1,0:T(8,128)} %get-tuple-element.24.side_second_ref), channel_id=1, source_target_pairs={{8,16},{24,32},{40,48},{56,64},{72,80},{88,96},{104,112},{16,8},{3... | collective-permute-start | bytes 737288 | tf_op jit(solution)/shard_map/ppermute | solution.py:769
  5.5 5.1 %copy-start.11 = (s32[2048]{0:T(1024)S(1)}, s32[2048]{0:T(1024)}, u32[]{:S(2)}) copy-start(s32[2048]{0:T(1024)} %param.15) | copy-start | bytes 24580
  5.5 5.1 %copy-start.5 = (s32[2048,1]{0,1:T(1,128)S(1)}, s32[2048,1]{0,1:T(1,128)}, u32[]{:S(2)}) copy-start(s32[2048,1]{0,1:T(1,128)} %param.16) | copy-start | bytes 24580
  5.5 5.1 %copy-start.9 = (f32[2048]{0:T(1024)S(1)}, f32[2048]{0:T(1024)}, u32[]{:S(2)}) copy-start(f32[2048]{0:T(1024)} %param.18) | copy-start | bytes 24580
  12.7 8.2 %collective-permute-start.2 = (f32[5,40,256]{2,1,0:T(8,128)S(1)}, f32[5,40,256]{2,1,0:T(8,128)S(1)}, u32[]{:S(2)}, u32[]{:S(2)}) collective-permute-start(f32[5,40,256]{2,1,0:T(8,128)S(1)} %get-tuple-element.27.line_first_ref), channel_id=1, source_target_pairs={{0,1},{1,0},{2,3},{3,2},{4,5},{5,4},{6,7},{7,6},{8,9},{9,8},{10,11... | collective-permute-start | bytes 614408 | tf_op jit(solution)/shard_map/ppermute | solution.py:769
  13.7 7.2 %collective-permute-start.3 = (f32[5,40,256]{2,1,0:T(8,128)S(1)}, f32[5,40,256]{2,1,0:T(8,128)S(1)}, u32[]{:S(2)}, u32[]{:S(2)}) collective-permute-start(f32[5,40,256]{2,1,0:T(8,128)S(1)} %get-tuple-element.28.line_second_ref), channel_id=1, source_target_pairs={{1,2},{3,4},{5,6},{2,1},{4,3},{6,5},{9,10},{11,12},{13,14},{10,9},... | collective-permute-start | bytes 614408 | tf_op jit(solution)/shard_map/ppermute | solution.py:769
  17.2 3.8 %copy-start.1 = (f32[32,48,256]{2,1,0:T(8,128)S(1)}, f32[32,48,256]{2,1,0:T(8,128)}, u32[]{:S(2)}) copy-start(f32[32,48,256]{2,1,0:T(8,128)} %storage_ref.5) | copy-start | bytes 4718596
  17.2 3.7 %copy-start.3 = (f32[5,48,256]{2,1,0:T(8,128)S(1)}, f32[5,48,256]{2,1,0:T(8,128)}, u32[]{:S(2)}) copy-start(f32[5,48,256]{2,1,0:T(8,128)} %get-tuple-element.23.side_first_ref) | copy-start | bytes 737284
  17.2 3.7 %copy-start.4 = (f32[5,48,256]{2,1,0:T(8,128)S(1)}, f32[5,48,256]{2,1,0:T(8,128)}, u32[]{:S(2)}) copy-start(f32[5,48,256]{2,1,0:T(8,128)} %get-tuple-element.24.side_second_ref) | copy-start | bytes 737284
  21.0 27.1 %copy-start.2 = (f32[4,768,768]{2,1,0:T(8,128)S(1)}, f32[4,768,768]{2,1,0:T(8,128)}, u32[]{:S(2)}) copy-start(f32[4,768,768]{2,1,0:T(8,128)} %matrix_ref.1) | copy-start | bytes 28311556
  21.0 27.0 %copy-start.6 = (s32[4,4,768]{2,1,0:T(4,128)S(1)}, s32[4,4,768]{2,1,0:T(4,128)}, u32[]{:S(2)}) copy-start(s32[4,4,768]{2,1,0:T(4,128)} %free_ref.1) | copy-start | bytes 147460
  21.0 27.0 %copy-start.7 = (f32[4,768]{1,0:T(4,128)S(1)}, f32[4,768]{1,0:T(4,128)}, u32[]{:S(2)}) copy-start(f32[4,768]{1,0:T(4,128)} %tectonic_ref.1) | copy-start | bytes 36868
  21.0 27.0 %copy-start.8 = (f32[4,768]{1,0:T(4,128)S(1)}, f32[4,768]{1,0:T(4,128)}, u32[]{:S(2)}) copy-start(f32[4,768]{1,0:T(4,128)} %yield_ref.1) | copy-start | bytes 36868
  21.0 27.0 %copy-start.10 = (s32[4,4]{1,0:T(4,128)S(1)}, s32[4,4]{1,0:T(4,128)}, u32[]{:S(2)}) copy-start(s32[4,4]{1,0:T(4,128)} %kind_ref.1) | copy-start | bytes 196

commit v4 on v3

--- a/solution.py
+++ b/solution.py
@@ -553,7 +553,6 @@
     wide,
     tall,
     turned,
-    rows,
     sem,
 ):
     patches, unknowns = tectonic_ref.shape
@@ -610,10 +609,17 @@
     piece_lane = lax.broadcasted_iota(jnp.int32, (16, patches * LANES), 1)
     choose = onehot((piece_row & 3) == (piece_lane >> 7))
 
+    place = lax.broadcasted_iota(jnp.int32, (8, unknowns), 0)
+
+    def fold(one, other, step):
+        return jnp.where(
+            place & step == 0, one + pltpu.roll(one, 8 - step, 0), other + pltpu.roll(other, step, 0)
+        )
+
     def times_matrix(vector):
         pieces = jnp.concatenate([*split3(vector), jnp.zeros_like(vector)], axis=0)
-        turned[...] = jnp.dot(
-            pieces.T.astype(jnp.bfloat16), choose, preferred_element_type=jnp.float32
+        turned[...] = lax.dot_general(
+            pieces.astype(jnp.bfloat16), choose, (((0,), (0,)), ((), ())), preferred_element_type=jnp.float32
         )
         group = 16
 
@@ -630,9 +636,9 @@
 
         zero = jnp.zeros((8, unknowns), jnp.float32)
         sums = lax.fori_loop(0, unknowns // (8 * group), body, (zero,) * patches)
-        for p in range(patches):
-            rows[p : p + 1, :] = jnp.sum(sums[p], axis=0, keepdims=True)
-        return rows[:patches, :]
+        low, high = fold(sums[0], sums[1], 1), fold(sums[2], sums[3], 1)
+        both = fold(low, high, 2)
+        return (both + pltpu.roll(both, 4, 0))[:patches]
 
     def mean(values):
         return jnp.sum(values, axis=1, keepdims=True) * (1.0 / unknowns)
@@ -687,7 +693,6 @@
             pltpu.VMEM((SLOTS * count, LANES), jnp.bfloat16),
             pltpu.VMEM((24 * tiles, SLOTS * count), jnp.bfloat16),
             pltpu.VMEM((unknowns, patches * LANES), jnp.float32),
-            pltpu.VMEM((8, unknowns), jnp.float32),
             pltpu.SemaphoreType.DMA,
         ],
         compiler_params=pltpu.CompilerParams(vmem_limit_bytes=20 * 2**20),
@@ -702,7 +707,7 @@
 WANTED = ((0, 0), (0, 1), (1, 0), (1, 1), (2, 0))
 
 
-def edges_kernel(source_ref, perm_ref, storage_ref, first_ref, second_ref, sems):
+def edges_kernel(source_ref, perm_ref, storage_ref, first_ref, second_ref, held, sems):
     planes = source_ref.shape[0]
     fields = (source_ref, perm_ref, storage_ref)
     even = is_even("cell")
@@ -711,22 +716,33 @@
         for k, out in enumerate((first_ref, second_ref)):
             at_end = even if k == 0 else 1 - even
             plane = deep + at_end * (planes - 1 - 2 * deep)
-            copies.append(pltpu.make_async_copy(fields[f].at[plane], out.at[n], sems.at[2 * n + k]))
-    for copy in copies:
-        copy.start()
-    for copy in copies:
-        copy.wait()
+            at = 2 * n + k
+            copies.append(
+                (
+                    pltpu.make_async_copy(fields[f].at[plane], held.at[at], sems.at[at]),
+                    pltpu.make_async_copy(held.at[at], out.at[n], sems.at[10 + at]),
+                )
+            )
+    for arriving, _ in copies:
+        arriving.start()
+    for arriving, leaving in copies:
+        arriving.wait()
+        leaving.start()
+    for _, leaving in copies:
+        leaving.wait()
 
 
 def edges(source, permeability, storage):
-    vmem = pl.BlockSpec(memory_space=pltpu.VMEM)
     side = jax.ShapeDtypeStruct((5,) + source.shape[1:], jnp.float32)
     return pl.pallas_call(
         edges_kernel,
         out_shape=(side, side),
         in_specs=[pl.BlockSpec(memory_space=pl.ANY)] * 3,
-        out_specs=(vmem,) * 2,
-        scratch_shapes=[pltpu.SemaphoreType.DMA((10,))],
+        out_specs=(pl.BlockSpec(memory_space=pl.ANY),) * 2,
+        scratch_shapes=[
+            pltpu.VMEM((10,) + source.shape[1:], jnp.float32),
+            pltpu.SemaphoreType.DMA((20,)),
+        ],
         compiler_params=pltpu.CompilerParams(vmem_limit_bytes=EDGES),
         name="edges",
     )(source, permeability, storage)

time: 59.5 us -> 59.1 us (level)
  no operation moved by 1% of the time
where the time goes in v4:
time: 59.1 us; the launch traced here: 58.9 us
  Pallas kernels  28.7 us (49%)
  blocking collectives  21.9 us (37%)
  starting transfers between devices  7.27 us (12%)
  between operations  0.92 us (2%)
    all_to_all x1, blocking collectives, on_device(): got = lax.all_to_all(sent, AXES, 0, 0, tiled=True)  21.9 us
    pallas_call x1, Pallas kernels, finish(): pl.pallas_call(functools.partial(final_kernel, step_kind.shape[0]), out_s...  10.9 us
    pallas_call x1, Pallas kernels, norms(): pl.pallas_call(norms_kernel, out_shape=(jax.ShapeDtypeStruct(source.shape...  5.11 us
    pallas_call x1, Pallas kernels, image_inside(): pl.pallas_call(image_kernel, out_shape=(block,) * 4 + (jax.ShapeDtypeStru...  5.08 us
    ppermute x2, starting transfers between devices, swap_pairs(): lax.ppermute(second_sent, axis, second)  4.11 us
    pallas_call x1, Pallas kernels, add_values(): pl.pallas_call(values_kernel, out_shape=jax.ShapeDtypeStruct((LANES, LANE...  3.69 us
    ppermute x2, starting transfers between devices, swap_pairs(): lax.ppermute(first_sent, axis, first)  3.17 us
    pallas_call x1, Pallas kernels, face_slots(): pl.pallas_call(slots_kernel, out_shape=(jax.ShapeDtypeStruct((LANES, LANE...  1.94 us
  transfers between devices with their start and end apart: 4, of which 0 were waited for; matrix products, arithmetic and copies ran while one was open for 0% of the time, Pallas kernels for 18%

profile of v4, /device:TPU:1, one launch (start us, length us, event | category | flops | bytes accessed | tf_op | source)
XLA Modules:
  0.0 58.9 jit_solution(11930948238022440812)
XLA Ops:
  0.6 1.9 %edges.1 = (f32[5,48,256]{2,1,0:T(8,128)}, f32[5,48,256]{2,1,0:T(8,128)}) custom-call(f32[32,48,256]{2,1,0:T(8,128)} %source_ref.7, f32[32,48,256]{2,1,0:T(8,128)} %perm_ref.3, f32[32,48,256]{2,1,0:T(8,128)} %storage_ref.5), custom_call_target="tpu_custom_call" | custom-call | tf_op jit(solution)/shard_map/edges/pallas_call | solution.py:737
  2.6 2.1 %collective-permute-start = (f32[5,48,256]{2,1,0:T(8,128)}, f32[5,48,256]{2,1,0:T(8,128)S(1)}, u32[]{:S(2)}, u32[]{:S(2)}) collective-permute-start(f32[5,48,256]{2,1,0:T(8,128)} %get-tuple-element.23.side_first_ref), channel_id=1, source_target_pairs={{0,8},{8,0},{16,24},{24,16},{32,40},{40,32},{48,56},{56,48},{64,72... | collective-permute-start | bytes 737288 | tf_op jit(solution)/shard_map/ppermute | solution.py:785
  4.7 0.7 %collective-permute-start.1 = (f32[5,48,256]{2,1,0:T(8,128)}, f32[5,48,256]{2,1,0:T(8,128)S(1)}, u32[]{:S(2)}, u32[]{:S(2)}) collective-permute-start(f32[5,48,256]{2,1,0:T(8,128)} %get-tuple-element.24.side_second_ref), channel_id=1, source_target_pairs={{8,16},{24,32},{40,48},{56,64},{72,80},{88,96},{104,112},{16,8},{3... | collective-permute-start | bytes 737288 | tf_op jit(solution)/shard_map/ppermute | solution.py:785
  5.4 0.0 copy-start.11
  5.4 0.0 copy-start.5
  5.5 0.0 copy-start.9
  5.5 5.1 %image.1 = (f32[32,48,256]{2,1,0:T(8,128)S(1)}, f32[32,48,256]{2,1,0:T(8,128)S(1)}, f32[32,48,256]{2,1,0:T(8,128)S(1)}, f32[32,48,256]{2,1,0:T(8,128)S(1)}, f32[...) custom-call(f32[32,48,256]{2,1,0:T(8,128)S(1)} %copy-done, f32[32,48,256]{2,1,0:T(8,128)} %perm_ref.3, ...), custom_call_target="tpu_custom_call" | custom-call | tf_op jit(solution)/shard_map/image/pallas_call | solution.py:304
  10.6 1.9 %slots.1 = (f32[128,128]{1,0:T(8,128)S(1)}, bf16[128,2048]{1,0:T(8,128)(2,1)S(1)}, f32[128,2048]{1,0:T(8,128)S(1)}, f32[3072,128]{1,0:T(8,128)S(1)}) custom-call(s32[16,128]{1,0:T(8,128)S(1)} %bitcast.13, f32[16,128]{1,0:T(8,128)S(1)} %fusion.8.code_ref, f32[16,128]{1,0:T(8,128)S(1)} %bitcast.17, s32[16,128]{1,0:T(8,128)S(1)} %get-tuple-element.36.lane_ref, ...), custom_call_target="tpu_custom_call" | custom-call | tf_op jit(solution)/shard_map/slots/pallas_call | solution.py:151
  12.6 0.0 collective-permute-done.one_ref.cell_first_ref
  12.6 1.0 %collective-permute-start.2 = (f32[5,40,256]{2,1,0:T(8,128)S(1)}, f32[5,40,256]{2,1,0:T(8,128)S(1)}, u32[]{:S(2)}, u32[]{:S(2)}) collective-permute-start(f32[5,40,256]{2,1,0:T(8,128)S(1)} %get-tuple-element.27.line_first_ref), channel_id=1, source_target_pairs={{0,1},{1,0},{2,3},{3,2},{4,5},{5,4},{6,7},{7,6},{8,9},{9,8},{10,11... | collective-permute-start | bytes 614408 | tf_op jit(solution)/shard_map/ppermute | solution.py:785
  13.7 3.4 %collective-permute-start.3 = (f32[5,40,256]{2,1,0:T(8,128)S(1)}, f32[5,40,256]{2,1,0:T(8,128)S(1)}, u32[]{:S(2)}, u32[]{:S(2)}) collective-permute-start(f32[5,40,256]{2,1,0:T(8,128)S(1)} %get-tuple-element.28.line_second_ref), channel_id=1, source_target_pairs={{1,2},{3,4},{5,6},{2,1},{4,3},{6,5},{9,10},{11,12},{13,14},{10,9},... | collective-permute-start | bytes 614408 | tf_op jit(solution)/shard_map/ppermute | solution.py:785
  17.1 0.0 copy-start.1
  17.1 0.0 copy-start.3
  17.1 3.7 %values.1.sent_in_ref = f32[128,128]{1,0:T(8,128)S(1)} custom-call(s32[2048]{0:T(1024)S(1)} %get-tuple-element.37.where_ref, s32[16,128]{1,0:T(8,128)S(1)} %bitcast.14, bf16[128,2048]{1,0:T(8,128)(2,1)S(1)} %get-tuple-element.19.slots_ref, f32[128,2048]{1,0:T(8,128)S(1)} %get-tuple-element.20.picker_ref, ...), custom_call_target="tpu_custom_call" | custom-call | tf_op jit(solution)/shard_map/values/pallas_call | solution.py:174
  20.8 0.0 collective-permute-done.2.sub_first_ref
  20.9 0.0 collective-permute-done.3.sub_second_ref
  20.9 0.0 copy-start.2
  20.9 0.0 copy-start.6
  20.9 0.0 copy-start.7
  20.9 0.0 copy-start.8
  20.9 0.0 copy-start.10
  21.0 5.1 %norms.1 = (f32[32,48,256]{2,1,0:T(8,128)S(1)}, f32[128,128]{1,0:T(8,128)S(1)}) custom-call(s32[2048]{0:T(1024)S(1)} %get-tuple-element.37.where_ref, s32[16,128]{1,0:T(8,128)S(1)} %bitcast.15, bf16[128,2048]{1,0:T(8,128)(2,1)S(1)} %get-tuple-element.19.slots_ref, f32[128,2048]{1,0:T(8,128)S(1)} %get-tuple-element.20.picker_ref, ...), custom_call_target="tpu_custom_call" | custom-call | tf_op jit(solution)/shard_map/norms/pallas_call | solution.py:518
  26.1 21.9 %all_to_all.11 = f32[128,1,128]{2,1,0:T(1,128)S(1)} all-to-all(f32[128,1,128]{2,1,0:T(1,128)S(1)} %bitcast.16), channel_id=1, replica_groups=mesh['cell'=16,'sub'=8] {'cell','sub'}, dimensions={0} | all-to-all | bytes 131072 | tf_op jit(solution)/shard_map/all_to_all | solution.py:822
  48.0 10.9 %finish.1 = (f32[32,48,256]{2,1,0:T(8,128)}, f32[4,768]{1,0:T(4,128)}) custom-call(s32[4,4]{1,0:T(4,128)S(1)} %copy-done.10, f32[128,128]{1,0:T(8,128)S(1)} %bitcast.12, f32[4,768]{1,0:T(4,128)S(1)} %copy-done.7, f32[4,768]{1,0:T(4,128)S(1)} %copy-done.8, s32[4,4,768]{2,1,0:T(4,128)S(1)} %copy-done.6, f32[4,768,768]{2,1,0:T(8,128)S(1)} %copy-done.2, ...), custom_call_target="tpu_custom_call" | custom-call | tf_op jit(solution)/shard_map/finish/pallas_call | solution.py:683
  (20 shorter events, 0.1 us)
Async XLA Ops:
  0.6 4.8 %copy-start = (f32[32,48,256]{2,1,0:T(8,128)S(1)}, f32[32,48,256]{2,1,0:T(8,128)}, u32[]{:S(2)}) copy-start(f32[32,48,256]{2,1,0:T(8,128)} %source_ref.7) | copy-start | bytes 4718596
  0.6 4.7 %copy-start.12 = (s32[2048]{0:T(1024)S(1)}, s32[2048]{0:T(1024)}, u32[]{:S(2)}) copy-start(s32[2048]{0:T(1024)} %param.17) | copy-start | bytes 24580
  2.6 10.0 %collective-permute-start = (f32[5,48,256]{2,1,0:T(8,128)}, f32[5,48,256]{2,1,0:T(8,128)S(1)}, u32[]{:S(2)}, u32[]{:S(2)}) collective-permute-start(f32[5,48,256]{2,1,0:T(8,128)} %get-tuple-element.23.side_first_ref), channel_id=1, source_target_pairs={{0,8},{8,0},{16,24},{24,16},{32,40},{40,32},{48,56},{56,48},{64,72... | collective-permute-start | bytes 737288 | tf_op jit(solution)/shard_map/ppermute | solution.py:785
  4.7 7.9 %collective-permute-start.1 = (f32[5,48,256]{2,1,0:T(8,128)}, f32[5,48,256]{2,1,0:T(8,128)S(1)}, u32[]{:S(2)}, u32[]{:S(2)}) collective-permute-start(f32[5,48,256]{2,1,0:T(8,128)} %get-tuple-element.24.side_second_ref), channel_id=1, source_target_pairs={{8,16},{24,32},{40,48},{56,64},{72,80},{88,96},{104,112},{16,8},{3... | collective-permute-start | bytes 737288 | tf_op jit(solution)/shard_map/ppermute | solution.py:785
  5.4 5.1 %copy-start.11 = (s32[2048]{0:T(1024)S(1)}, s32[2048]{0:T(1024)}, u32[]{:S(2)}) copy-start(s32[2048]{0:T(1024)} %param.15) | copy-start | bytes 24580
  5.4 5.1 %copy-start.5 = (s32[2048,1]{0,1:T(1,128)S(1)}, s32[2048,1]{0,1:T(1,128)}, u32[]{:S(2)}) copy-start(s32[2048,1]{0,1:T(1,128)} %param.16) | copy-start | bytes 24580
  5.5 5.1 %copy-start.9 = (f32[2048]{0:T(1024)S(1)}, f32[2048]{0:T(1024)}, u32[]{:S(2)}) copy-start(f32[2048]{0:T(1024)} %param.18) | copy-start | bytes 24580
  12.6 8.2 %collective-permute-start.2 = (f32[5,40,256]{2,1,0:T(8,128)S(1)}, f32[5,40,256]{2,1,0:T(8,128)S(1)}, u32[]{:S(2)}, u32[]{:S(2)}) collective-permute-start(f32[5,40,256]{2,1,0:T(8,128)S(1)} %get-tuple-element.27.line_first_ref), channel_id=1, source_target_pairs={{0,1},{1,0},{2,3},{3,2},{4,5},{5,4},{6,7},{7,6},{8,9},{9,8},{10,11... | collective-permute-start | bytes 614408 | tf_op jit(solution)/shard_map/ppermute | solution.py:785
  13.7 7.2 %collective-permute-start.3 = (f32[5,40,256]{2,1,0:T(8,128)S(1)}, f32[5,40,256]{2,1,0:T(8,128)S(1)}, u32[]{:S(2)}, u32[]{:S(2)}) collective-permute-start(f32[5,40,256]{2,1,0:T(8,128)S(1)} %get-tuple-element.28.line_second_ref), channel_id=1, source_target_pairs={{1,2},{3,4},{5,6},{2,1},{4,3},{6,5},{9,10},{11,12},{13,14},{10,9},... | collective-permute-start | bytes 614408 | tf_op jit(solution)/shard_map/ppermute | solution.py:785
  17.1 3.8 %copy-start.1 = (f32[32,48,256]{2,1,0:T(8,128)S(1)}, f32[32,48,256]{2,1,0:T(8,128)}, u32[]{:S(2)}) copy-start(f32[32,48,256]{2,1,0:T(8,128)} %storage_ref.5) | copy-start | bytes 4718596
  17.1 3.8 %copy-start.3 = (f32[5,48,256]{2,1,0:T(8,128)S(1)}, f32[5,48,256]{2,1,0:T(8,128)}, u32[]{:S(2)}) copy-start(f32[5,48,256]{2,1,0:T(8,128)} %get-tuple-element.23.side_first_ref) | copy-start | bytes 737284
  17.1 3.7 %copy-start.4 = (f32[5,48,256]{2,1,0:T(8,128)S(1)}, f32[5,48,256]{2,1,0:T(8,128)}, u32[]{:S(2)}) copy-start(f32[5,48,256]{2,1,0:T(8,128)} %get-tuple-element.24.side_second_ref) | copy-start | bytes 737284
  20.9 27.1 %copy-start.2 = (f32[4,768,768]{2,1,0:T(8,128)S(1)}, f32[4,768,768]{2,1,0:T(8,128)}, u32[]{:S(2)}) copy-start(f32[4,768,768]{2,1,0:T(8,128)} %matrix_ref.1) | copy-start | bytes 28311556
  20.9 27.0 %copy-start.6 = (s32[4,4,768]{2,1,0:T(4,128)S(1)}, s32[4,4,768]{2,1,0:T(4,128)}, u32[]{:S(2)}) copy-start(s32[4,4,768]{2,1,0:T(4,128)} %free_ref.1) | copy-start | bytes 147460
  20.9 27.0 %copy-start.7 = (f32[4,768]{1,0:T(4,128)S(1)}, f32[4,768]{1,0:T(4,128)}, u32[]{:S(2)}) copy-start(f32[4,768]{1,0:T(4,128)} %tectonic_ref.1) | copy-start | bytes 36868
  20.9 27.0 %copy-start.8 = (f32[4,768]{1,0:T(4,128)S(1)}, f32[4,768]{1,0:T(4,128)}, u32[]{:S(2)}) copy-start(f32[4,768]{1,0:T(4,128)} %yield_ref.1) | copy-start | bytes 36868
  20.9 27.0 %copy-start.10 = (s32[4,4]{1,0:T(4,128)S(1)}, s32[4,4]{1,0:T(4,128)}, u32[]{:S(2)}) copy-start(s32[4,4]{1,0:T(4,128)} %kind_ref.1) | copy-start | bytes 196
